TPU v7x, 256 devices: a whole 4x4x8 slice. The times are simulated.
256 devices in a mesh: dp: 16 (over z, y_hi), fsdp: 16 (over y_lo, x, core).
Axes of the slice: x: 4, y: 4 (y_hi: 2, y_lo: 2; y = y_hi * 2 + y_lo), z: 8, core: 2. Of those that a mesh axis runs over, the one named last changes fastest.
Arguments:
- activations: bfloat16 [131072, 4096], P(('dp', 'fsdp')), may hold values from -6 to 6
- cotangent: bfloat16 [131072, 4096], P(('dp', 'fsdp')), may hold values from -0.0625 to 0.0625
- basis: bfloat16 [4096, 1024], P('fsdp'), may hold values from -0.09375 to 0.09375
- weight: bfloat16 [4096, 4096], P(None, 'fsdp'), may hold values from -6 to 6
- first: float32 [1024, 16, 16, 16], P(None, 'fsdp', 'dp'), may hold values from -6 to 6
- second: float32 [1024, 16, 16, 16], P(None, 'fsdp', 'dp'), may hold values from 0.25 to 4
Outputs:
- new_weight: bfloat16 [4096, 4096], P(None, 'fsdp')
- new_first: float32 [1024, 16, 16, 16], P(None, 'fsdp', 'dp')
- new_second: float32 [1024, 16, 16, 16], P(None, 'fsdp', 'dp')
All inputs are finite; a program needn't handle non-finite values.
Results may differ from a plain program's by a relative error of at most 0.0045.
Values may be sent and summed in bfloat16 or wider, within the bound.
No kernel may reach another device: no remote copies, remote signals or barrier semaphores. Data moves between devices by JAX's collectives and lax.ppermute only.
A program may use at most 128 MiB of HBM per device.

v0:
```python
import math

import jax
import jax.numpy as jnp
import numpy as np
from jax import lax
from jax.experimental import pallas as pl
from jax.experimental.pallas import tpu as pltpu
from jax.sharding import PartitionSpec as P

beta_one = 0.9
beta_two = 0.999
corr_one = 1.0 - math.exp(1000.0 * math.log(0.9))
corr_two = 1.0 - math.exp(1000.0 * math.log(0.999))
epsilon = 1e-08
rate = 0.5

AXES = ("dp", "fsdp")
NX, NY, NZ = 4, 4, 8
SMALL, LARGE = 16 * 2**20, 56 * 2**20


def place(x, y, z, c):
    return (z * 2 + y // 2) * 16 + ((y % 2) * 4 + x) * 2 + c


CHIPS = [(x, y, z) for z in range(NZ) for y in range(NY) for x in range(NX)]


def route(value, where):
    pairs = []
    for x, y, z in CHIPS:
        for c in range(2):
            tx, ty, tz, tc = where(x, y, z, c)
            pairs.append((place(x, y, z, c), place(tx % NX, ty % NY, tz % NZ, tc)))
    return lax.ppermute(value, AXES, sorted(pairs))


def swap(value):
    return route(value, lambda x, y, z, c: (x, y, z, 1 - c))


def ring_x(value):
    return route(value, lambda x, y, z, c: (x + 1 - 2 * c, y, z, c))


def ring_y(value):
    return route(value, lambda x, y, z, c: (x, y + 1 - 2 * c, z, c))


def along(value, by, first):
    return route(
        value,
        lambda x, y, z, c: (x + by, y, z, c) if (c == 0) == first else (x, y + by, z, c),
    )


def together(*values):
    return lax.optimization_barrier(values)


def along_zc():
    return [
        [place(x, y, z, c) for z in range(NZ) for c in range(2)]
        for y in range(NY)
        for x in range(NX)
    ]


def exchange(value, groups):
    return lax.all_to_all(value, AXES, 0, 0, tiled=True, axis_index_groups=groups)


def dot(a, b, dims):
    return lax.dot_general(a, b, (dims, ((), ())), preferred_element_type=jnp.float32)


HBM = pl.BlockSpec(memory_space=pltpu.HBM)
LOCAL = pl.BlockSpec(memory_space=pltpu.VMEM)
EITHER = pl.BlockSpec(memory_space=pl.ANY)


def run(kernel, table, args, outs, scratch, copies, flops, moved, local=(), pinned=(), vmem=SMALL):
    where = {i: LOCAL for i in local} | {i: HBM for i in pinned}
    return pl.pallas_call(
        kernel,
        grid_spec=pltpu.PrefetchScalarGridSpec(
            num_scalar_prefetch=1,
            grid=(),
            in_specs=[where.get(i, EITHER) for i in range(len(args))],
            out_specs=[HBM] * len(outs),
            scratch_shapes=[pltpu.VMEM(shape, dtype) for shape, dtype in scratch]
            + [pltpu.SemaphoreType.DMA((copies,))],
        ),
        out_shape=outs,
        cost_estimate=pl.CostEstimate(flops=flops, bytes_accessed=moved, transcendentals=0),
        compiler_params=pltpu.CompilerParams(vmem_limit_bytes=vmem),
    )(table, *args)


class Copies:
    def __init__(self, sems):
        self.sems, self.used = sems, 0

    def __call__(self, source, target):
        copy = pltpu.make_async_copy(source, target, self.sems.at[self.used])
        self.used += 1
        copy.start()
        return copy


def fetch_pieces(copies, table, phase, own, other, pieces, blocks, basis):
    half, (depth, low_rank) = own.shape[0], pieces[0].shape
    low, started = low_rank // 2, []
    lanes = pl.ds(pl.multiple_of(table[CORE] * low, low), low)
    for j, piece in enumerate(pieces):
        at = pl.ds(j * depth, depth)
        columns = pl.ds(pl.multiple_of(table[PIECES[phase] + j] * depth, depth), depth)
        started += [
            copies(own.at[:, columns], blocks.at[:half, at]),
            copies(other.at[:, columns], blocks.at[half:, at]),
            copies(piece.at[:, lanes], basis.at[at, :]),
        ]
    return started


def wait(copies):
    for copy in copies:
        copy.wait()


def project(table, phase, own, other, pieces, before=None, vmem=SMALL):
    n, half = len(pieces), own.shape[0]
    depth, low = pieces[0].shape[0], pieces[0].shape[1] // 2
    total = jax.ShapeDtypeStruct((2 * half, low), jnp.float32)
    extra = [] if before is None else [before]

    def kernel(table, own, other, *refs):
        pieces, (out, blocks, basis, total, sems) = refs[:n], refs[-5:]
        copies = Copies(sems)
        started = fetch_pieces(copies, table, phase, own, other, pieces, blocks, basis)
        if extra:
            started.append(copies(refs[n], total))
        wait(started)
        ended = []
        for m in range(4):
            rows = pl.ds(m * half // 2, half // 2)
            part = dot(blocks[rows, :], basis[...], ((1,), (0,)))
            total[rows, :] = total[rows, :] + part if extra else part
            ended.append(copies(total.at[rows, :], out.at[rows, :]))
        wait(ended)

    return run(
        kernel,
        table,
        (own, other, *pieces, *extra),
        [total],
        [
            ((2 * half, n * depth), jnp.bfloat16),
            ((n * depth, low), jnp.bfloat16),
            (total.shape, jnp.float32),
        ],
        3 * n + 5,
        4 * half * depth * n * low,
        n * 2**20,
        pinned=(0,),
        vmem=vmem,
    )[0]


def write_tiles(sems, table, call, near, far, projected, dealt, outs):
    def each_out(j, h, act):
        at = TILES[call] + 5 * j + 1 + 2 * h
        for w, out in enumerate(outs):

            @pl.when(table[at] == w)
            def _(out=out):
                target = out.at[table[at + 1]]
                act(pltpu.make_async_copy(dealt.at[j, h], target, sems.at[2 * j + h]))

    for j in range(4):
        cols, half = near.shape[1] // 8, near.shape[0]
        at = table[TILES[call] + 5 * j]
        columns = pl.ds(pl.multiple_of(at * cols, cols), cols)
        total = dot(near[:, columns], projected[:half, :], ((0,), (0,)))
        total += dot(far[:, columns], projected[half:, :], ((0,), (0,)))
        total = total.astype(jnp.bfloat16)
        for h in range(2):
            for z in range(NZ):
                for c in range(2):
                    row = c * 256 + z * 32 + h * 16
                    to = z * 32 + c * 16
                    dealt[j, h, to : to + 16, :] = total[row : row + 16, :]
            each_out(j, h, lambda copy: copy.start())
    for j in range(4):
        for h in range(2):
            each_out(j, h, lambda copy: copy.wait())


def gradient_shapes(near, low):
    half, width = near.shape
    cols = width // 8
    slots = jax.ShapeDtypeStruct((2, cols // 2, low), jnp.bfloat16)
    scratch = [
        ((2 * half, low), jnp.bfloat16),
        ((4, 2, cols // 2, low), jnp.bfloat16),
    ]
    return slots, scratch


def finish(table, own, other, pieces, before, near, far):
    half, width = own.shape
    n, depth, low = len(pieces), pieces[0].shape[0], pieces[0].shape[1] // 2
    slots, scratch = gradient_shapes(near, low)

    def kernel(table, own, other, *refs):
        pieces, (before, near, far, out) = refs[:n], refs[n : n + 4]
        outs, (blocks, basis, projected, dealt, sems) = refs[n + 4 : -5], refs[-5:]
        copies = Copies(sems.at[pl.ds(8, 3 * n + 2)])
        started = fetch_pieces(copies, table, 2, own, other, pieces, blocks, basis)
        wait(started)
        for m in range(4):
            rows = pl.ds(m * half // 2, half // 2)
            part = dot(blocks[rows, :], basis[...], ((1,), (0,)))
            projected[rows, :] = (before[rows, :] + part).astype(projected.dtype)
        kept = copies(projected, out)
        write_tiles(sems, table, 0, near, far, projected, dealt, outs)
        kept.wait()

    return run(
        kernel,
        table,
        (own, other, *pieces, before, near, far),
        [jax.ShapeDtypeStruct((2 * half, low), jnp.bfloat16)] + [slots] * 4,
        [
            ((2 * half, n * depth), jnp.bfloat16),
            ((n * depth, low), jnp.bfloat16),
            *scratch,
        ],
        3 * n + 10,
        2 * half * width * low,
        11 * 2**20,
        local=(n + 2, n + 3, n + 4),
        pinned=(0,),
    )


def gradient(table, near, far, projected):
    half, width = near.shape
    low = projected.shape[1]
    slots, scratch = gradient_shapes(near, low)

    def kernel(table, near, far, source, *refs):
        outs, (projected, dealt, sems) = refs[:4], refs[4:]
        Copies(sems.at[pl.ds(8, 1)])(source, projected).wait()
        write_tiles(sems, table, 1, near, far, projected, dealt, outs)

    return run(
        kernel,
        table,
        (near, far, projected),
        [slots] * 4,
        scratch,
        9,
        2 * half * width * low,
        7 * 2**20,
        local=(0, 1),
    )


def expand(table, mine, rest, update, weight):
    depth, low_rank = mine[0].shape
    cols = weight.shape[1]
    n = len(mine)

    def kernel(table, *refs):
        pieces, (factor, weight, out, new, sems) = refs[: 2 * n], refs[2 * n :]
        copies = Copies(sems)
        ended = []
        for j in range(n):
            for i, side in ((j, table[CORE]), (n + j, 1 - table[CORE])):
                at = pl.multiple_of((2 * table[SHARDS + j] + side) * depth, depth)
                rows = pl.ds(at, depth)
                total = dot(pieces[i][...], factor[...], ((1,), (1,)))
                new[i] = (weight[rows, :].astype(jnp.float32) - rate * total).astype(new.dtype)
                ended.append(copies(new.at[i], out.at[rows, :]))
        wait(ended)

    args = (*mine, *rest, update, weight)
    return run(
        kernel,
        table,
        args,
        [jax.ShapeDtypeStruct(weight.shape, weight.dtype)],
        [((2 * n, depth, cols), jnp.bfloat16)],
        2 * n,
        2 * weight.size * low_rank,
        13 * 2**20,
        local=range(len(args)),
    )[0]


def added(*values):
    return sum(v.astype(jnp.float32) for v in values).astype(jnp.bfloat16)


def tile_rows(core, x, y, call):
    low, rows = y % 2, []
    for j in range(4):
        if core == 0:
            rows.append((j % 2) * 4 + (x + ((2, 0), (1, 3))[call][j // 2]) % 4)
            for h in range(2):
                slot = (h * 2 + j % 2 - y) % 4
                rows += [j // 2 * 2 + slot // 2, slot % 2]
        else:
            side = low if call == 0 else 1 - low
            rows.append(side * 4 + (x + j) % 4)
            for h in range(2):
                which = int((h * 2 + side - y) % 4 != 2 - call)
                rows += [which * 2 + j // 2, j % 2]
    return rows


TURNED = [4 * (j // 4) + (4 - j) % 4 for j in range(8)]
PHASES = ((0, 1, 4), (2, 5, 3, 6), (7,))
CORE, SHARDS, TILES, PIECES = 0, 1, (9, 29), (49, 55, 63)


def device_row(x, y, core):
    shards = [((y + j // 4) % 2) * 4 + (x + (2 * core - 1) * j) % 4 for j in range(8)]
    row = [core] + shards
    for call in range(2):
        row += tile_rows(core, x, y, call)
    for phase in PHASES:
        for j in phase:
            row += [2 * shards[j] + core, 2 * shards[TURNED[j]] + 1 - core]
    return row


def device_table():
    rows = {place(x, y, z, c): device_row(x, y, c) for x, y, z in CHIPS for c in range(2)}
    return np.array([rows[i] for i in range(len(rows))], np.int32)


def body(activations, cotangent, basis, weight, first, second):
    low_rank = basis.shape[1]
    half = low_rank // 2
    owned = first.shape[-1]
    f, d = lax.axis_index("fsdp"), lax.axis_index("dp")
    table = lax.dynamic_index_in_dim(device_table(), d * 16 + f, 0, keepdims=False)

    other_activations, s_x0, y0, x1 = together(
        swap(activations), swap(basis), ring_y(basis), ring_x(basis)
    )
    s_y0, s_x1, y1, x2, x1, y0 = together(
        swap(y0), swap(x1), ring_y(x1), ring_x(x1), x1, y0
    )
    both = (activations, other_activations)
    begun = project(table, 0, *both, [basis, s_x0, x1, s_x1, y0, s_y0], vmem=LARGE)
    s_y1, s_x2, y2, x3, begun, x2, y1, cotangent = together(
        swap(y1), swap(x2), ring_y(x2), ring_x(x2), begun, x2, y1, cotangent
    )
    cotangent, s_x3, s_y2 = together(cotangent, swap(x3), swap(y2))
    other_cotangent = swap(cotangent)
    begun = project(table, 1, *both, [x2, s_x2, y1, s_y1, x3, s_x3, y2, s_y2], begun, SMALL)
    other_cotangent, y3, begun = together(other_cotangent, ring_y(x3), begun)
    s_y3 = swap(y3)
    projected, *opposite_own = finish(
        table, *both, (y3, s_y3), begun, cotangent, other_cotangent
    )
    mine = (basis, x1, x2, x3, y0, y1, y2, y3)
    rest = (s_x0, s_x1, s_x2, s_x3, s_y0, s_y1, s_y2, s_y3)
    rest = tuple(rest[j] for j in TURNED)

    opposite_a, opposite_b, own_a, own_b = opposite_own
    came_a, came_b = along(opposite_a, 1, True), along(opposite_b, -1, True)
    next_a, next_b, last_a, last_b = gradient(table, cotangent, other_cotangent, projected)
    next_b, last_a = along(next_b, 1, True), along(last_a, -1, True)
    next_a = along(added(next_a, came_a), 1, True)
    last_b = along(added(last_b, came_b), -1, True)
    own, following, opposite, previous = [
        added(*(t[i] for t in terms))
        for terms in ((own_a, next_a, last_a), (own_b, next_b, last_b))
        for i in range(2)
    ]
    terms = added(
        own,
        along(opposite, 2, False),
        along(following, 1, False),
        along(previous, -1, False),
    )
    terms = exchange(terms.reshape(16, owned, half), along_zc())
    summed = jnp.sum(terms.reshape(NZ, 2, owned, half).astype(jnp.float32), axis=0)
    summed = summed.transpose(1, 0, 2).reshape(owned, low_rank)

    moment_one = beta_one * first.reshape(low_rank, owned).T + (1.0 - beta_one) * summed
    moment_two = beta_two * second.reshape(low_rank, owned).T + (1.0 - beta_two) * summed * summed
    update = moment_one / corr_one / (jnp.sqrt(moment_two / corr_two) + epsilon)
    update = update.astype(jnp.bfloat16)
    copies = jnp.broadcast_to(update[None], (16, owned, low_rank))
    update = lax.all_to_all(copies, "dp", 0, 0, tiled=True).reshape(16 * owned, low_rank)

    new_weight = expand(table, mine, rest, update, weight)
    return (new_weight, moment_one.T.reshape(first.shape), moment_two.T.reshape(first.shape))


def solution(mesh):
    in_specs = (
        P(("dp", "fsdp"), None),
        P(("dp", "fsdp"), None),
        P("fsdp", None),
        P(None, "fsdp"),
        P(None, "fsdp", "dp", None),
        P(None, "fsdp", "dp", None),
    )
    out_specs = (P(None, "fsdp"), P(None, "fsdp", "dp", None), P(None, "fsdp", "dp", None))
    return jax.shard_map(body, mesh=mesh, in_specs=in_specs, out_specs=out_specs, check_vma=False)
```

profile of v0, /device:TPU:8, one launch (start us, length us, event | category | flops | bytes accessed | tf_op | source)
XLA Modules:
  0.0 142.7 jit_solution(10721800479388121444)
XLA Ops:
  0.7 1.6 %collective-permute-start.3 = (bf16[256,1024]{1,0:T(8,128)(2,1)}, bf16[256,1024]{1,0:T(8,128)(2,1)S(1)}, u32[]{:S(2)}, u32[]{:S(2)}) collective-permute-start(bf16[256,1024]{1,0:T(8,128)(2,1)} %refs_0_.3), channel_id=1, source_target_pairs={{0,2},{1,7},{2,4},{3,1},{4,6},{5,3},{6,0},{7,5},{8,10},{9,15},{10,... | collective-permute-start | bytes 1572872 | tf_op jit(solution)/shard_map/ppermute | solution.py:36
  2.3 1.6 %collective-permute-start.2 = (bf16[256,1024]{1,0:T(8,128)(2,1)}, bf16[256,1024]{1,0:T(8,128)(2,1)S(1)}, u32[]{:S(2)}, u32[]{:S(2)}) collective-permute-start(bf16[256,1024]{1,0:T(8,128)(2,1)} %refs_0_.3), channel_id=1, source_target_pairs={{0,8},{1,25},{2,10},{3,27},{4,12},{5,29},{6,14},{7,31},{8,16},{9,1... | collective-permute-start | bytes 1572872 | tf_op jit(solution)/shard_map/ppermute | solution.py:36
  3.9 7.5 %collective-permute-done.3.refs_2_.refs_1_ = bf16[256,1024]{1,0:T(8,128)(2,1)S(1)} collective-permute-done((bf16[256,1024]{1,0:T(8,128)(2,1)}, bf16[256,1024]{1,0:T(8,128)(2,1)S(1)}, u32[]{:S(2)}, u32[]{:S(2)}) %collective-permute-start.3) | collective-permute-done | bytes 524320 | tf_op jit(solution)/shard_map/ppermute | solution.py:36
  11.4 0.3 collective-permute-done.2.refs_4_
  11.7 0.3 collective-permute-start.4
  12.0 1.3 collective-permute-start.7
  13.4 1.6 %collective-permute-start.6 = (bf16[256,1024]{1,0:T(8,128)(2,1)S(1)}, bf16[256,1024]{1,0:T(8,128)(2,1)S(1)}, u32[]{:S(2)}, u32[]{:S(2)}) collective-permute-start(bf16[256,1024]{1,0:T(8,128)(2,1)S(1)} %collective-permute-done.3.refs_2_.refs_1_), channel_id=1, source_target_pairs={{0,8},{1,25},{2,10},{3,27},{4,12},{5,29},{6,14},{7,31},{8,16},{9,1... | collective-permute-start | bytes 1572872 | tf_op jit(solution)/shard_map/ppermute | solution.py:36
  15.0 1.9 %collective-permute-start.5 = (bf16[256,1024]{1,0:T(8,128)(2,1)S(1)}, bf16[256,1024]{1,0:T(8,128)(2,1)S(1)}, u32[]{:S(2)}, u32[]{:S(2)}) collective-permute-start(bf16[256,1024]{1,0:T(8,128)(2,1)S(1)} %collective-permute-done.3.refs_2_.refs_1_), channel_id=1, source_target_pairs={{0,1},{1,0},{2,3},{3,2},{4,5},{5,4},{6,7},{7,6},{8,9},{9,8},{10,11... | collective-permute-start | bytes 1572872 | tf_op jit(solution)/shard_map/ppermute | solution.py:36
  16.9 5.5 %collective-permute-done.7.refs_0_.refs_2_ = bf16[256,1024]{1,0:T(8,128)(2,1)S(1)} collective-permute-done((bf16[256,1024]{1,0:T(8,128)(2,1)S(1)}, bf16[256,1024]{1,0:T(8,128)(2,1)S(1)}, u32[]{:S(2)}, u32[]{:S(2)}) %collective-permute-start.7) | collective-permute-done | bytes 524320 | tf_op jit(solution)/shard_map/ppermute | solution.py:36
  22.6 0.5 collective-permute-start.8
  23.0 0.8 collective-permute-start.11
  23.8 1.6 %collective-permute-start.10 = (bf16[256,1024]{1,0:T(8,128)(2,1)S(1)}, bf16[256,1024]{1,0:T(8,128)(2,1)S(1)}, u32[]{:S(2)}, u32[]{:S(2)}) collective-permute-start(bf16[256,1024]{1,0:T(8,128)(2,1)S(1)} %collective-permute-done.7.refs_0_.refs_2_), channel_id=1, source_target_pairs={{0,8},{1,25},{2,10},{3,27},{4,12},{5,29},{6,14},{7,31},{8,16},{9,1... | collective-permute-start | bytes 1572872 | tf_op jit(solution)/shard_map/ppermute | solution.py:36
  25.4 2.0 %collective-permute-start.9 = (bf16[256,1024]{1,0:T(8,128)(2,1)S(1)}, bf16[256,1024]{1,0:T(8,128)(2,1)S(1)}, u32[]{:S(2)}, u32[]{:S(2)}) collective-permute-start(bf16[256,1024]{1,0:T(8,128)(2,1)S(1)} %collective-permute-done.7.refs_0_.refs_2_), channel_id=1, source_target_pairs={{0,1},{1,0},{2,3},{3,2},{4,5},{5,4},{6,7},{7,6},{8,9},{9,8},{10,11... | collective-permute-start | bytes 1572872 | tf_op jit(solution)/shard_map/ppermute | solution.py:36
  27.5 1.2 dynamic-slice_bitcast_fusion.table
  28.7 6.3 %shard_map.94.refs_8_ = f32[1024,512]{1,0:T(8,128)} custom-call(s32[65]{0:T(128)} %dynamic-slice_bitcast_fusion.table, bf16[512,4096]{1,0:T(8,128)(2,1)} %own.5, bf16[512,4096]{1,0:T(8,128)(2,1)} %collective-permute-done.other, bf16[256,1024]{1,0:T(8,128)(2,1)} %refs_0_.3, bf16[256,1024]{1,0:T(8,128)(2,1)} %copy-done.9, bf16[256,1024]{1,0:T(8,128)(2,1)} %copy-done.5, ...), custom_call_target="tpu_custom_call" | custom-call | flops 1610612736 | bytes 6291456 | tf_op jit(solution)/shard_map/pallas_call | solution.py:85
  35.1 0.1 collective-permute-start.13
  35.2 0.5 collective-permute-start.12
  35.7 1.4 collective-permute-done.13.refs_7_.refs_14_
  37.1 0.7 collective-permute-done.12.refs_5_.refs_9_
  37.8 0.1 collective-permute-start.14
  38.1 1.6 %copy-done.2 = f32[1024,512]{1,0:T(8,128)S(1)} copy-done((f32[1024,512]{1,0:T(8,128)S(1)}, f32[1024,512]{1,0:T(8,128)}, u32[]{:S(2)}) %copy-start.2) | copy-done | bytes 2097176
  39.6 5.4 %shard_map.95.refs_2_ = f32[1024,512]{1,0:T(8,128)S(1)} custom-call(s32[65]{0:T(128)S(1)} %copy-done.15, bf16[512,4096]{1,0:T(8,128)(2,1)S(1)} %copy-done, bf16[512,4096]{1,0:T(8,128)(2,1)} %collective-permute-done.other, bf16[256,1024]{1,0:T(8,128)(2,1)S(1)} %collective-permute-done.7.refs_0_.refs_2_, ...), custom_call_target="tpu_custom_call" | custom-call | flops 2147483648 | bytes 8388608 | tf_op jit(solution)/shard_map/pallas_call | solution.py:85
  45.1 2.0 %collective-permute-done.15.refs_0_.refs_7_ = bf16[256,1024]{1,0:T(8,128)(2,1)S(1)} collective-permute-done((bf16[256,1024]{1,0:T(8,128)(2,1)S(1)}, bf16[256,1024]{1,0:T(8,128)(2,1)S(1)}, u32[]{:S(2)}, u32[]{:S(2)}) %collective-permute-start.15) | collective-permute-done | bytes 524320 | tf_op jit(solution)/shard_map/ppermute | solution.py:36
  47.2 1.9 %collective-permute-done.16.refs_1_.refs_13_ = bf16[256,1024]{1,0:T(8,128)(2,1)S(1)} collective-permute-done((bf16[256,1024]{1,0:T(8,128)(2,1)S(1)}, bf16[256,1024]{1,0:T(8,128)(2,1)S(1)}, u32[]{:S(2)}, u32[]{:S(2)}) %collective-permute-start.16) | collective-permute-done | bytes 524320 | tf_op jit(solution)/shard_map/ppermute | solution.py:36
  49.0 6.2 %shard_map.96 = (bf16[1024,512]{1,0:T(8,128)(2,1)S(1)}, bf16[2,256,512]{2,1,0:T(8,128)(2,1)S(1)}, bf16[2,256,512]{2,1,0:T(8,128)(2,1)S(1)}, bf16[2,256,512]{2,1,0:T(8,128)(2,1)S(1)}, bf16[2,256,512]{2,1,0:T(8,128)(2,1)S(1)}) custom-call(s32[65]{0:T(128)S(1)} %copy-done.15, bf16[512,4096]{1,0:T(8,128)(2,1)S(1)} %copy-done, ...), custom_call_target="tpu_custom_call" | custom-call | flops 2147483648 | bytes 11534336 | tf_op jit(solution)/shard_map/pallas_call | solution.py:85
  55.2 2.2 %collective-permute-start.17 = (bf16[2,256,512]{2,1,0:T(8,128)(2,1)S(1)}, bf16[2,256,512]{2,1,0:T(8,128)(2,1)S(1)}, u32[]{:S(2)}, u32[]{:S(2)}) collective-permute-start(bf16[2,256,512]{2,1,0:T(8,128)(2,1)S(1)} %get-tuple-element.63), channel_id=1, source_target_pairs={{0,2},{1,9},{2,4},{3,11},{4,6},{5,13},{6,0},{7,15},{8,10},{9,17},{... | collective-permute-start | bytes 1572872 | tf_op jit(solution)/shard_map/ppermute | solution.py:36
  57.5 1.1 collective-permute-start.21
  58.6 4.3 %shard_map.97 = (bf16[2,256,512]{2,1,0:T(8,128)(2,1)S(1)}, bf16[2,256,512]{2,1,0:T(8,128)(2,1)S(1)}, bf16[2,256,512]{2,1,0:T(8,128)(2,1)S(1)}, bf16[2,256,512]{2,1,0:T(8,128)(2,1)S(1)}) custom-call(s32[65]{0:T(128)S(1)} %copy-done.15, bf16[512,4096]{1,0:T(8,128)(2,1)S(1)} %copy-done.1, bf16[512,4096]{1,0:T(8,128)(2,1)S(1)} %collective-permute-done.14.refs_4_.far, ...), custom_call_target="tpu_custom_call" | custom-call | flops 2147483648 | bytes 7340032 | tf_op jit(solution)/shard_map/pallas_call | solution.py:85
  62.9 0.8 collective-permute-start.19
  63.7 1.3 collective-permute-start.20
  65.0 0.7 collective-permute-done.17
  65.7 0.1 add_convert_fusion.1
  65.8 1.0 collective-permute-start.18
  66.9 0.1 add_convert_fusion
  67.1 2.4 %collective-permute-start.22 = (bf16[2,256,512]{2,1,0:T(8,128)(2,1)S(1)}, bf16[2,256,512]{2,1,0:T(8,128)(2,1)S(1)}, u32[]{:S(2)}, u32[]{:S(2)}) collective-permute-start(bf16[2,256,512]{2,1,0:T(8,128)(2,1)S(1)} %add_convert_fusion), channel_id=1, source_target_pairs={{0,6},{1,25},{2,0},{3,27},{4,2},{5,29},{6,4},{7,31},{8,14},{9,1},{... | collective-permute-start | bytes 1572872 | tf_op jit(solution)/shard_map/ppermute | solution.py:36
  69.5 2.8 %collective-permute-done.19 = bf16[2,256,512]{2,1,0:T(8,128)(2,1)S(1)} collective-permute-done((bf16[2,256,512]{2,1,0:T(8,128)(2,1)S(1)}, bf16[2,256,512]{2,1,0:T(8,128)(2,1)S(1)}, u32[]{:S(2)}, u32[]{:S(2)}) %collective-permute-start.19) | collective-permute-done | bytes 524320 | tf_op jit(solution)/shard_map/ppermute | solution.py:36
  72.3 7.5 %collective-permute-done.18 = bf16[2,256,512]{2,1,0:T(8,128)(2,1)S(1)} collective-permute-done((bf16[2,256,512]{2,1,0:T(8,128)(2,1)S(1)}, bf16[2,256,512]{2,1,0:T(8,128)(2,1)S(1)}, u32[]{:S(2)}, u32[]{:S(2)}) %collective-permute-start.18) | collective-permute-done | bytes 524320 | tf_op jit(solution)/shard_map/ppermute | solution.py:36
  79.8 0.9 collective-permute-start.24
  80.8 0.2 fusion.4
  81.0 4.5 %collective-permute-start.23 = (bf16[256,512]{1,0:T(8,128)(2,1)S(1)}, bf16[256,512]{1,0:T(8,128)(2,1)S(1)}, u32[]{:S(2)}, u32[]{:S(2)}) collective-permute-start(bf16[256,512]{1,0:T(8,128)(2,1)S(1)} %get-tuple-element.69), channel_id=1, source_target_pairs={{0,16},{1,5},{2,18},{3,7},{4,20},{5,1},{6,22},{7,3},{8,24},{9,13},... | collective-permute-start | bytes 786440 | tf_op jit(solution)/shard_map/ppermute | solution.py:36
  85.5 2.0 %collective-permute-done.24 = bf16[256,512]{1,0:T(8,128)(2,1)S(1)} collective-permute-done((bf16[256,512]{1,0:T(8,128)(2,1)S(1)}, bf16[256,512]{1,0:T(8,128)(2,1)S(1)}, u32[]{:S(2)}, u32[]{:S(2)}) %collective-permute-start.24) | collective-permute-done | bytes 262176 | tf_op jit(solution)/shard_map/ppermute | solution.py:36
  87.5 2.5 %collective-permute-done.23 = bf16[256,512]{1,0:T(8,128)(2,1)S(1)} collective-permute-done((bf16[256,512]{1,0:T(8,128)(2,1)S(1)}, bf16[256,512]{1,0:T(8,128)(2,1)S(1)}, u32[]{:S(2)}, u32[]{:S(2)}) %collective-permute-start.23) | collective-permute-done | bytes 262176 | tf_op jit(solution)/shard_map/ppermute | solution.py:36
  90.0 2.7 %collective-permute-done.25 = bf16[256,512]{1,0:T(8,128)(2,1)S(1)} collective-permute-done((bf16[256,512]{1,0:T(8,128)(2,1)S(1)}, bf16[256,512]{1,0:T(8,128)(2,1)S(1)}, u32[]{:S(2)}, u32[]{:S(2)}) %collective-permute-start.25) | collective-permute-done | bytes 262176 | tf_op jit(solution)/shard_map/ppermute | solution.py:36
  92.7 0.2 fusion.2
  92.9 19.6 %all_to_all.10 = bf16[16,16,512]{2,1,0:T(8,128)(2,1)S(1)} all-to-all(bf16[16,16,512]{2,1,0:T(8,128)(2,1)S(1)} %bitcast.45), channel_id=1, replica_groups={{0,1,32,33,64,65,96,97,128,129,160,161,192,193,224,225},{2,3,34,35,66,6..., dimensions={0} | all-to-all | bytes 524288 | tf_op jit(solution)/shard_map/all_to_all | solution.py:71
  112.5 0.7 fusion.9
  113.3 25.4 %all_to_all.11 = bf16[16,16,1024]{2,1,0:T(8,128)(2,1)S(1)} all-to-all(bf16[16,16,1024]{2,1,0:T(8,128)(2,1)S(1)} %broadcast_in_dim.2), channel_id=1, replica_groups=mesh['dp'=16,'fsdp'=16] {'dp'}, dimensions={0} | all-to-all | bytes 1048576 | tf_op jit(solution)/shard_map/all_to_all | solution.py:401
  138.7 3.8 %shard_map.98 = bf16[4096,256]{1,0:T(8,128)(2,1)} custom-call(s32[65]{0:T(128)S(1)} %copy-done.15, bf16[256,1024]{1,0:T(8,128)(2,1)S(1)} %copy-done.4, bf16[256,1024]{1,0:T(8,128)(2,1)S(1)} %copy-done.6, bf16[256,1024]{1,0:T(8,128)(2,1)S(1)} %collective-permute-done.7.refs_0_.refs_2_, bf16[256,1024]{1,0:T(8,128)(2,1)S(1)} %collective-permute-done.11.refs_4_.refs_3_, ...), custom_call_target="tpu_custom_call" | custom-call | flops 2147483648 | bytes 13631488 | tf_op jit(solution)/shard_map/pallas_call | solution.py:85
  (57 shorter events, 0.7 us)
Async XLA Ops:
  0.6 11.1 %collective-permute-start = (bf16[512,4096]{1,0:T(8,128)(2,1)}, bf16[512,4096]{1,0:T(8,128)(2,1)}, u32[]{:S(2)}, u32[]{:S(2)}) collective-permute-start(bf16[512,4096]{1,0:T(8,128)(2,1)} %own.5), channel_id=1, source_target_pairs={{0,1},{1,0},{2,3},{3,2},{4,5},{5,4},{6,7},{7,6},{8,9},{9,8},{10,11... | collective-permute-start | bytes 12582920 | tf_op jit(solution)/shard_map/ppermute | solution.py:36
  0.7 10.7 %collective-permute-start.3 = (bf16[256,1024]{1,0:T(8,128)(2,1)}, bf16[256,1024]{1,0:T(8,128)(2,1)S(1)}, u32[]{:S(2)}, u32[]{:S(2)}) collective-permute-start(bf16[256,1024]{1,0:T(8,128)(2,1)} %refs_0_.3), channel_id=1, source_target_pairs={{0,2},{1,7},{2,4},{3,1},{4,6},{5,3},{6,0},{7,5},{8,10},{9,15},{10,... | collective-permute-start | bytes 1572872 | tf_op jit(solution)/shard_map/ppermute | solution.py:36
  2.3 9.4 %collective-permute-start.2 = (bf16[256,1024]{1,0:T(8,128)(2,1)}, bf16[256,1024]{1,0:T(8,128)(2,1)S(1)}, u32[]{:S(2)}, u32[]{:S(2)}) collective-permute-start(bf16[256,1024]{1,0:T(8,128)(2,1)} %refs_0_.3), channel_id=1, source_target_pairs={{0,8},{1,25},{2,10},{3,27},{4,12},{5,29},{6,14},{7,31},{8,16},{9,1... | collective-permute-start | bytes 1572872 | tf_op jit(solution)/shard_map/ppermute | solution.py:36
  3.9 7.8 %collective-permute-start.1 = (bf16[256,1024]{1,0:T(8,128)(2,1)}, bf16[256,1024]{1,0:T(8,128)(2,1)S(1)}, u32[]{:S(2)}, u32[]{:S(2)}) collective-permute-start(bf16[256,1024]{1,0:T(8,128)(2,1)} %refs_0_.3), channel_id=1, source_target_pairs={{0,1},{1,0},{2,3},{3,2},{4,5},{5,4},{6,7},{7,6},{8,9},{9,8},{10,11... | collective-permute-start | bytes 1572872 | tf_op jit(solution)/shard_map/ppermute | solution.py:36
  11.4 12.4 %copy-start.5 = (bf16[256,1024]{1,0:T(8,128)(2,1)}, bf16[256,1024]{1,0:T(8,128)(2,1)S(1)}, u32[]{:S(2)}) copy-start(bf16[256,1024]{1,0:T(8,128)(2,1)S(1)} %collective-permute-done.3.refs_2_.refs_1_) | copy-start | bytes 1572868
  11.7 13.7 %copy-start.7 = (bf16[256,1024]{1,0:T(8,128)(2,1)}, bf16[256,1024]{1,0:T(8,128)(2,1)S(1)}, u32[]{:S(2)}) copy-start(bf16[256,1024]{1,0:T(8,128)(2,1)S(1)} %collective-permute-done.2.refs_4_) | copy-start | bytes 1572868
  11.7 15.8 %copy-start.9 = (bf16[256,1024]{1,0:T(8,128)(2,1)}, bf16[256,1024]{1,0:T(8,128)(2,1)S(1)}, u32[]{:S(2)}) copy-start(bf16[256,1024]{1,0:T(8,128)(2,1)S(1)} %collective-permute-done.1.refs_1_.refs_8_) | copy-start | bytes 1572868
  11.7 5.2 %collective-permute-start.4 = (bf16[256,1024]{1,0:T(8,128)(2,1)S(1)}, bf16[256,1024]{1,0:T(8,128)(2,1)S(1)}, u32[]{:S(2)}, u32[]{:S(2)}) collective-permute-start(bf16[256,1024]{1,0:T(8,128)(2,1)S(1)} %collective-permute-done.2.refs_4_), channel_id=1, source_target_pairs={{0,1},{1,0},{2,3},{3,2},{4,5},{5,4},{6,7},{7,6},{8,9},{9,8},{10,11... | collective-permute-start | bytes 1572872 | tf_op jit(solution)/shard_map/ppermute | solution.py:36
  12.0 10.4 %collective-permute-start.7 = (bf16[256,1024]{1,0:T(8,128)(2,1)S(1)}, bf16[256,1024]{1,0:T(8,128)(2,1)S(1)}, u32[]{:S(2)}, u32[]{:S(2)}) collective-permute-start(bf16[256,1024]{1,0:T(8,128)(2,1)S(1)} %collective-permute-done.3.refs_2_.refs_1_), channel_id=1, source_target_pairs={{0,2},{1,7},{2,4},{3,1},{4,6},{5,3},{6,0},{7,5},{8,10},{9,15},{10,... | collective-permute-start | bytes 1572872 | tf_op jit(solution)/shard_map/ppermute | solution.py:36
  13.4 9.2 %collective-permute-start.6 = (bf16[256,1024]{1,0:T(8,128)(2,1)S(1)}, bf16[256,1024]{1,0:T(8,128)(2,1)S(1)}, u32[]{:S(2)}, u32[]{:S(2)}) collective-permute-start(bf16[256,1024]{1,0:T(8,128)(2,1)S(1)} %collective-permute-done.3.refs_2_.refs_1_), channel_id=1, source_target_pairs={{0,8},{1,25},{2,10},{3,27},{4,12},{5,29},{6,14},{7,31},{8,16},{9,1... | collective-permute-start | bytes 1572872 | tf_op jit(solution)/shard_map/ppermute | solution.py:36
  15.0 7.6 %collective-permute-start.5 = (bf16[256,1024]{1,0:T(8,128)(2,1)S(1)}, bf16[256,1024]{1,0:T(8,128)(2,1)S(1)}, u32[]{:S(2)}, u32[]{:S(2)}) collective-permute-start(bf16[256,1024]{1,0:T(8,128)(2,1)S(1)} %collective-permute-done.3.refs_2_.refs_1_), channel_id=1, source_target_pairs={{0,1},{1,0},{2,3},{3,2},{4,5},{5,4},{6,7},{7,6},{8,9},{9,8},{10,11... | collective-permute-start | bytes 1572872 | tf_op jit(solution)/shard_map/ppermute | solution.py:36
  16.9 10.6 %copy-start.11 = (bf16[256,1024]{1,0:T(8,128)(2,1)}, bf16[256,1024]{1,0:T(8,128)(2,1)S(1)}, u32[]{:S(2)}) copy-start(bf16[256,1024]{1,0:T(8,128)(2,1)S(1)} %collective-permute-done.4.refs_5_.refs_12_) | copy-start | bytes 1572868
  22.6 4.9 %copy-start.13 = (bf16[256,1024]{1,0:T(8,128)(2,1)}, bf16[256,1024]{1,0:T(8,128)(2,1)S(1)}, u32[]{:S(2)}) copy-start(bf16[256,1024]{1,0:T(8,128)(2,1)S(1)} %collective-permute-done.5.refs_3_.refs_11_) | copy-start | bytes 1572868
  22.6 12.5 %collective-permute-start.8 = (bf16[256,1024]{1,0:T(8,128)(2,1)S(1)}, bf16[256,1024]{1,0:T(8,128)(2,1)S(1)}, u32[]{:S(2)}, u32[]{:S(2)}) collective-permute-start(bf16[256,1024]{1,0:T(8,128)(2,1)S(1)} %collective-permute-done.6.refs_2_.refs_5_), channel_id=1, source_target_pairs={{0,1},{1,0},{2,3},{3,2},{4,5},{5,4},{6,7},{7,6},{8,9},{9,8},{10,11... | collective-permute-start | bytes 1572872 | tf_op jit(solution)/shard_map/ppermute | solution.py:36
  23.0 12.0 %collective-permute-start.11 = (bf16[256,1024]{1,0:T(8,128)(2,1)S(1)}, bf16[256,1024]{1,0:T(8,128)(2,1)S(1)}, u32[]{:S(2)}, u32[]{:S(2)}) collective-permute-start(bf16[256,1024]{1,0:T(8,128)(2,1)S(1)} %collective-permute-done.7.refs_0_.refs_2_), channel_id=1, source_target_pairs={{0,2},{1,7},{2,4},{3,1},{4,6},{5,3},{6,0},{7,5},{8,10},{9,15},{10,... | collective-permute-start | bytes 1572872 | tf_op jit(solution)/shard_map/ppermute | solution.py:36
  23.8 11.2 %collective-permute-start.10 = (bf16[256,1024]{1,0:T(8,128)(2,1)S(1)}, bf16[256,1024]{1,0:T(8,128)(2,1)S(1)}, u32[]{:S(2)}, u32[]{:S(2)}) collective-permute-start(bf16[256,1024]{1,0:T(8,128)(2,1)S(1)} %collective-permute-done.7.refs_0_.refs_2_), channel_id=1, source_target_pairs={{0,8},{1,25},{2,10},{3,27},{4,12},{5,29},{6,14},{7,31},{8,16},{9,1... | collective-permute-start | bytes 1572872 | tf_op jit(solution)/shard_map/ppermute | solution.py:36
  25.4 9.6 %collective-permute-start.9 = (bf16[256,1024]{1,0:T(8,128)(2,1)S(1)}, bf16[256,1024]{1,0:T(8,128)(2,1)S(1)}, u32[]{:S(2)}, u32[]{:S(2)}) collective-permute-start(bf16[256,1024]{1,0:T(8,128)(2,1)S(1)} %collective-permute-done.7.refs_0_.refs_2_), channel_id=1, source_target_pairs={{0,1},{1,0},{2,3},{3,2},{4,5},{5,4},{6,7},{7,6},{8,9},{9,8},{10,11... | collective-permute-start | bytes 1572872 | tf_op jit(solution)/shard_map/ppermute | solution.py:36
  28.7 9.4 %copy-start = (bf16[512,4096]{1,0:T(8,128)(2,1)S(1)}, bf16[512,4096]{1,0:T(8,128)(2,1)}, u32[]{:S(2)}) copy-start(bf16[512,4096]{1,0:T(8,128)(2,1)} %own.5) | copy-start | bytes 12582916
  28.7 9.4 %copy-start.15 = (s32[65]{0:T(128)S(1)}, s32[65]{0:T(128)}, u32[]{:S(2)}) copy-start(s32[65]{0:T(128)} %dynamic-slice_bitcast_fusion.table) | copy-start | bytes 784
  35.0 14.0 %copy-start.1 = (bf16[512,4096]{1,0:T(8,128)(2,1)S(1)}, bf16[512,4096]{1,0:T(8,128)(2,1)}, u32[]{:S(2)}) copy-start(bf16[512,4096]{1,0:T(8,128)(2,1)} %near) | copy-start | bytes 12582916
  35.1 2.0 %collective-permute-start.13 = (bf16[256,1024]{1,0:T(8,128)(2,1)S(1)}, bf16[256,1024]{1,0:T(8,128)(2,1)S(1)}, u32[]{:S(2)}, u32[]{:S(2)}) collective-permute-start(bf16[256,1024]{1,0:T(8,128)(2,1)S(1)} %collective-permute-done.10.refs_6_), channel_id=1, source_target_pairs={{0,1},{1,0},{2,3},{3,2},{4,5},{5,4},{6,7},{7,6},{8,9},{9,8},{10,11... | collective-permute-start | bytes 1572872 | tf_op jit(solution)/shard_map/ppermute | solution.py:36
  35.2 2.6 %collective-permute-start.12 = (bf16[256,1024]{1,0:T(8,128)(2,1)S(1)}, bf16[256,1024]{1,0:T(8,128)(2,1)S(1)}, u32[]{:S(2)}, u32[]{:S(2)}) collective-permute-start(bf16[256,1024]{1,0:T(8,128)(2,1)S(1)} %collective-permute-done.11.refs_4_.refs_3_), channel_id=1, source_target_pairs={{0,1},{1,0},{2,3},{3,2},{4,5},{5,4},{6,7},{7,6},{8,9},{9,8},{10,11... | collective-permute-start | bytes 1572872 | tf_op jit(solution)/shard_map/ppermute | solution.py:36
  37.8 9.3 %collective-permute-start.14 = (bf16[512,4096]{1,0:T(8,128)(2,1)}, bf16[512,4096]{1,0:T(8,128)(2,1)S(1)}, u32[]{:S(2)}, u32[]{:S(2)}) collective-permute-start(bf16[512,4096]{1,0:T(8,128)(2,1)} %near), channel_id=1, source_target_pairs={{0,1},{1,0},{2,3},{3,2},{4,5},{5,4},{6,7},{7,6},{8,9},{9,8},{10,11... | collective-permute-start | bytes 12582920 | tf_op jit(solution)/shard_map/ppermute | solution.py:36
  37.9 9.2 %collective-permute-start.15 = (bf16[256,1024]{1,0:T(8,128)(2,1)S(1)}, bf16[256,1024]{1,0:T(8,128)(2,1)S(1)}, u32[]{:S(2)}, u32[]{:S(2)}) collective-permute-start(bf16[256,1024]{1,0:T(8,128)(2,1)S(1)} %collective-permute-done.11.refs_4_.refs_3_), channel_id=1, source_target_pairs={{0,8},{1,25},{2,10},{3,27},{4,12},{5,29},{6,14},{7,31},{8,16},{9,1... | collective-permute-start | bytes 1572872 | tf_op jit(solution)/shard_map/ppermute | solution.py:36
  38.1 1.6 %copy-start.2 = (f32[1024,512]{1,0:T(8,128)S(1)}, f32[1024,512]{1,0:T(8,128)}, u32[]{:S(2)}) copy-start(f32[1024,512]{1,0:T(8,128)} %shard_map.94.refs_8_) | copy-start | bytes 6291460
  47.1 1.9 %collective-permute-start.16 = (bf16[256,1024]{1,0:T(8,128)(2,1)S(1)}, bf16[256,1024]{1,0:T(8,128)(2,1)S(1)}, u32[]{:S(2)}, u32[]{:S(2)}) collective-permute-start(bf16[256,1024]{1,0:T(8,128)(2,1)S(1)} %collective-permute-done.15.refs_0_.refs_7_), channel_id=1, source_target_pairs={{0,1},{1,0},{2,3},{3,2},{4,5},{5,4},{6,7},{7,6},{8,9},{9,8},{10,11... | collective-permute-start | bytes 1572872 | tf_op jit(solution)/shard_map/ppermute | solution.py:36
  55.2 10.5 %collective-permute-start.17 = (bf16[2,256,512]{2,1,0:T(8,128)(2,1)S(1)}, bf16[2,256,512]{2,1,0:T(8,128)(2,1)S(1)}, u32[]{:S(2)}, u32[]{:S(2)}) collective-permute-start(bf16[2,256,512]{2,1,0:T(8,128)(2,1)S(1)} %get-tuple-element.63), channel_id=1, source_target_pairs={{0,2},{1,9},{2,4},{3,11},{4,6},{5,13},{6,0},{7,15},{8,10},{9,17},{... | collective-permute-start | bytes 1572872 | tf_op jit(solution)/shard_map/ppermute | solution.py:36
  57.5 9.4 %collective-permute-start.21 = (bf16[2,256,512]{2,1,0:T(8,128)(2,1)S(1)}, bf16[2,256,512]{2,1,0:T(8,128)(2,1)S(1)}, u32[]{:S(2)}, u32[]{:S(2)}) collective-permute-start(bf16[2,256,512]{2,1,0:T(8,128)(2,1)S(1)} %get-tuple-element.68), channel_id=1, source_target_pairs={{0,6},{1,25},{2,0},{3,27},{4,2},{5,29},{6,4},{7,31},{8,14},{9,1},{... | collective-permute-start | bytes 1572872 | tf_op jit(solution)/shard_map/ppermute | solution.py:36
  62.9 9.4 %collective-permute-start.19 = (bf16[2,256,512]{2,1,0:T(8,128)(2,1)S(1)}, bf16[2,256,512]{2,1,0:T(8,128)(2,1)S(1)}, u32[]{:S(2)}, u32[]{:S(2)}) collective-permute-start(bf16[2,256,512]{2,1,0:T(8,128)(2,1)S(1)} %get-tuple-element.64), channel_id=1, source_target_pairs={{0,6},{1,25},{2,0},{3,27},{4,2},{5,29},{6,4},{7,31},{8,14},{9,1},{... | collective-permute-start | bytes 1572872 | tf_op jit(solution)/shard_map/ppermute | solution.py:36
  63.7 17.0 %collective-permute-start.20 = (bf16[2,256,512]{2,1,0:T(8,128)(2,1)S(1)}, bf16[2,256,512]{2,1,0:T(8,128)(2,1)S(1)}, u32[]{:S(2)}, u32[]{:S(2)}) collective-permute-start(bf16[2,256,512]{2,1,0:T(8,128)(2,1)S(1)} %get-tuple-element.66), channel_id=1, source_target_pairs={{0,2},{1,9},{2,4},{3,11},{4,6},{5,13},{6,0},{7,15},{8,10},{9,17},{... | collective-permute-start | bytes 1572872 | tf_op jit(solution)/shard_map/ppermute | solution.py:36
  65.7 46.8 %copy-start.16 = (f32[1024,1,1,16]{0,3,2,1:T(8,128)S(1)}, f32[1024,1,1,16]{0,3,2,1:T(8,128)}, u32[]{:S(2)}) copy-start(f32[1024,1,1,16]{0,3,2,1:T(8,128)} %param.12) | copy-start | bytes 196612
  65.7 46.8 %copy-start.17 = (f32[1024,1,1,16]{0,3,2,1:T(8,128)S(1)}, f32[1024,1,1,16]{0,3,2,1:T(8,128)}, u32[]{:S(2)}) copy-start(f32[1024,1,1,16]{0,3,2,1:T(8,128)} %param.11) | copy-start | bytes 196612
  65.8 13.9 %collective-permute-start.18 = (bf16[2,256,512]{2,1,0:T(8,128)(2,1)S(1)}, bf16[2,256,512]{2,1,0:T(8,128)(2,1)S(1)}, u32[]{:S(2)}, u32[]{:S(2)}) collective-permute-start(bf16[2,256,512]{2,1,0:T(8,128)(2,1)S(1)} %add_convert_fusion.1), channel_id=1, source_target_pairs={{0,2},{1,9},{2,4},{3,11},{4,6},{5,13},{6,0},{7,15},{8,10},{9,17},{... | collective-permute-start | bytes 1572872 | tf_op jit(solution)/shard_map/ppermute | solution.py:36
  67.0 71.6 %copy-start.3 = (bf16[4096,256]{1,0:T(8,128)(2,1)S(1)}, bf16[4096,256]{1,0:T(8,128)(2,1)}, u32[]{:S(2)}) copy-start(bf16[4096,256]{1,0:T(8,128)(2,1)} %refs_17_.1) | copy-start | bytes 6291460
  67.0 71.6 %copy-start.4 = (bf16[256,1024]{1,0:T(8,128)(2,1)S(1)}, bf16[256,1024]{1,0:T(8,128)(2,1)}, u32[]{:S(2)}) copy-start(bf16[256,1024]{1,0:T(8,128)(2,1)} %refs_0_.3) | copy-start | bytes 1572868
  67.0 71.6 %copy-start.6 = (bf16[256,1024]{1,0:T(8,128)(2,1)S(1)}, bf16[256,1024]{1,0:T(8,128)(2,1)}, u32[]{:S(2)}) copy-start(bf16[256,1024]{1,0:T(8,128)(2,1)} %copy-done.5) | copy-start | bytes 1572868
  67.0 71.6 %copy-start.8 = (bf16[256,1024]{1,0:T(8,128)(2,1)S(1)}, bf16[256,1024]{1,0:T(8,128)(2,1)}, u32[]{:S(2)}) copy-start(bf16[256,1024]{1,0:T(8,128)(2,1)} %copy-done.7) | copy-start | bytes 1572868
  67.0 71.6 %copy-start.10 = (bf16[256,1024]{1,0:T(8,128)(2,1)S(1)}, bf16[256,1024]{1,0:T(8,128)(2,1)}, u32[]{:S(2)}) copy-start(bf16[256,1024]{1,0:T(8,128)(2,1)} %copy-done.9) | copy-start | bytes 1572868
  67.1 71.6 %copy-start.12 = (bf16[256,1024]{1,0:T(8,128)(2,1)S(1)}, bf16[256,1024]{1,0:T(8,128)(2,1)}, u32[]{:S(2)}) copy-start(bf16[256,1024]{1,0:T(8,128)(2,1)} %copy-done.11) | copy-start | bytes 1572868
  67.1 71.6 %copy-start.14 = (bf16[256,1024]{1,0:T(8,128)(2,1)S(1)}, bf16[256,1024]{1,0:T(8,128)(2,1)}, u32[]{:S(2)}) copy-start(bf16[256,1024]{1,0:T(8,128)(2,1)} %copy-done.13) | copy-start | bytes 1572868
  67.1 13.7 %collective-permute-start.22 = (bf16[2,256,512]{2,1,0:T(8,128)(2,1)S(1)}, bf16[2,256,512]{2,1,0:T(8,128)(2,1)S(1)}, u32[]{:S(2)}, u32[]{:S(2)}) collective-permute-start(bf16[2,256,512]{2,1,0:T(8,128)(2,1)S(1)} %add_convert_fusion), channel_id=1, source_target_pairs={{0,6},{1,25},{2,0},{3,27},{4,2},{5,29},{6,4},{7,31},{8,14},{9,1},{... | collective-permute-start | bytes 1572872 | tf_op jit(solution)/shard_map/ppermute | solution.py:36
  79.8 7.7 %collective-permute-start.24 = (bf16[256,512]{1,0:T(8,128)(2,1)S(1)}, bf16[256,512]{1,0:T(8,128)(2,1)S(1)}, u32[]{:S(2)}, u32[]{:S(2)}) collective-permute-start(bf16[256,512]{1,0:T(8,128)(2,1)S(1)} %fusion.5), channel_id=1, source_target_pairs={{0,8},{1,3},{2,10},{3,5},{4,12},{5,7},{6,14},{7,1},{8,16},{9,11},{... | collective-permute-start | bytes 786440 | tf_op jit(solution)/shard_map/ppermute | solution.py:36
  81.0 9.0 %collective-permute-start.23 = (bf16[256,512]{1,0:T(8,128)(2,1)S(1)}, bf16[256,512]{1,0:T(8,128)(2,1)S(1)}, u32[]{:S(2)}, u32[]{:S(2)}) collective-permute-start(bf16[256,512]{1,0:T(8,128)(2,1)S(1)} %get-tuple-element.69), channel_id=1, source_target_pairs={{0,16},{1,5},{2,18},{3,7},{4,20},{5,1},{6,22},{7,3},{8,24},{9,13},... | collective-permute-start | bytes 786440 | tf_op jit(solution)/shard_map/ppermute | solution.py:36
  85.5 7.2 %collective-permute-start.25 = (bf16[256,512]{1,0:T(8,128)(2,1)S(1)}, bf16[256,512]{1,0:T(8,128)(2,1)S(1)}, u32[]{:S(2)}, u32[]{:S(2)}) collective-permute-start(bf16[256,512]{1,0:T(8,128)(2,1)S(1)} %get-tuple-element.70), channel_id=1, source_target_pairs={{0,24},{1,7},{2,26},{3,1},{4,28},{5,3},{6,30},{7,5},{8,0},{9,15},{... | collective-permute-start | bytes 786440 | tf_op jit(solution)/shard_map/ppermute | solution.py:36
where the time goes:
time: 143 us
  blocking collectives  44.9 us (31%)
  waiting for transfers between devices  37.7 us (26%)
  starting transfers between devices  28.5 us (20%)
  Pallas kernels  26.1 us (18%)
  local copies, waits for them, and re-layouts  2.92 us (2%)
  other arithmetic  1.5 us (1%)
    ppermute x26, waiting for transfers between devices, route(): return lax.ppermute(value, AXES, sorted(pairs))  37.7 us
    ppermute x26, starting transfers between devices, route(): return lax.ppermute(value, AXES, sorted(pairs))  28.5 us
    pallas_call x5, Pallas kernels, run(): pl.pallas_call(kernel, grid_spec=pltpu.PrefetchScalarGridSpec(num_scalar_...  26.1 us
    all_to_all x1, blocking collectives, body(): lax.all_to_all(copies, 'dp', 0, 0, tiled=True).reshape(16 * owned, low_rank)  25.4 us
    all_to_all x1, blocking collectives, exchange(): lax.all_to_all(value, AXES, 0, 0, tiled=True, axis_index_groups=groups)  19.6 us
  transfers between devices with their start and end apart: 26, of which 14 were waited for; matrix products, arithmetic and copies ran while one was open for 1% of the time, Pallas kernels for 11%

commit v1 on v0

--- a/solution.py
+++ b/solution.py
@@ -80,7 +80,7 @@
 EITHER = pl.BlockSpec(memory_space=pl.ANY)
 
 
-def run(kernel, table, args, outs, scratch, copies, flops, moved, local=(), pinned=(), vmem=SMALL):
+def run(kernel, table, args, outs, scratch, copies, flops, moved, local=(), pinned=(), vmem=SMALL, here=False):
     where = {i: LOCAL for i in local} | {i: HBM for i in pinned}
     return pl.pallas_call(
         kernel,
@@ -88,7 +88,7 @@
             num_scalar_prefetch=1,
             grid=(),
             in_specs=[where.get(i, EITHER) for i in range(len(args))],
-            out_specs=[HBM] * len(outs),
+            out_specs=[LOCAL if here else HBM] * len(outs),
             scratch_shapes=[pltpu.VMEM(shape, dtype) for shape, dtype in scratch]
             + [pltpu.SemaphoreType.DMA((copies,))],
         ),
@@ -109,7 +109,7 @@
         return copy
 
 
-def fetch_pieces(copies, table, phase, own, other, pieces, blocks, basis):
+def fetch_pieces(copies, table, phase, own, other, pieces, blocks, basis=None):
     half, (depth, low_rank) = own.shape[0], pieces[0].shape
     low, started = low_rank // 2, []
     lanes = pl.ds(pl.multiple_of(table[CORE] * low, low), low)
@@ -119,8 +119,9 @@
         started += [
             copies(own.at[:, columns], blocks.at[:half, at]),
             copies(other.at[:, columns], blocks.at[half:, at]),
-            copies(piece.at[:, lanes], basis.at[at, :]),
         ]
+        if basis is not None:
+            started.append(copies(piece.at[:, lanes], basis.at[at, :]))
     return started
 
 
@@ -129,38 +130,33 @@
         copy.wait()
 
 
-def project(table, phase, own, other, pieces, before=None, vmem=SMALL):
+def project(table, phase, own, other, pieces, vmem=SMALL):
     n, half = len(pieces), own.shape[0]
     depth, low = pieces[0].shape[0], pieces[0].shape[1] // 2
     total = jax.ShapeDtypeStruct((2 * half, low), jnp.float32)
-    extra = [] if before is None else [before]
 
     def kernel(table, own, other, *refs):
-        pieces, (out, blocks, basis, total, sems) = refs[:n], refs[-5:]
+        pieces, (out, blocks, basis, total, sems) = refs[:n], refs[n:]
         copies = Copies(sems)
-        started = fetch_pieces(copies, table, phase, own, other, pieces, blocks, basis)
-        if extra:
-            started.append(copies(refs[n], total))
-        wait(started)
+        wait(fetch_pieces(copies, table, phase, own, other, pieces, blocks, basis))
         ended = []
         for m in range(4):
             rows = pl.ds(m * half // 2, half // 2)
-            part = dot(blocks[rows, :], basis[...], ((1,), (0,)))
-            total[rows, :] = total[rows, :] + part if extra else part
+            total[rows, :] = dot(blocks[rows, :], basis[...], ((1,), (0,)))
             ended.append(copies(total.at[rows, :], out.at[rows, :]))
         wait(ended)
 
     return run(
         kernel,
         table,
-        (own, other, *pieces, *extra),
+        (own, other, *pieces),
         [total],
         [
             ((2 * half, n * depth), jnp.bfloat16),
             ((n * depth, low), jnp.bfloat16),
             (total.shape, jnp.float32),
         ],
-        3 * n + 5,
+        3 * n + 4,
         4 * half * depth * n * low,
         n * 2**20,
         pinned=(0,),
@@ -168,79 +164,69 @@
     )[0]
 
 
-def write_tiles(sems, table, call, near, far, projected, dealt, outs):
-    def each_out(j, h, act):
-        at = TILES[call] + 5 * j + 1 + 2 * h
-        for w, out in enumerate(outs):
-
-            @pl.when(table[at] == w)
-            def _(out=out):
-                target = out.at[table[at + 1]]
-                act(pltpu.make_async_copy(dealt.at[j, h], target, sems.at[2 * j + h]))
-
+def write_tiles(table, call, near, far, projected, outs):
     for j in range(4):
         cols, half = near.shape[1] // 8, near.shape[0]
-        at = table[TILES[call] + 5 * j]
-        columns = pl.ds(pl.multiple_of(at * cols, cols), cols)
+        at = TILES[call] + 5 * j
+        columns = pl.ds(pl.multiple_of(table[at] * cols, cols), cols)
         total = dot(near[:, columns], projected[:half, :], ((0,), (0,)))
         total += dot(far[:, columns], projected[half:, :], ((0,), (0,)))
         total = total.astype(jnp.bfloat16)
         for h in range(2):
-            for z in range(NZ):
-                for c in range(2):
-                    row = c * 256 + z * 32 + h * 16
-                    to = z * 32 + c * 16
-                    dealt[j, h, to : to + 16, :] = total[row : row + 16, :]
-            each_out(j, h, lambda copy: copy.start())
-    for j in range(4):
-        for h in range(2):
-            each_out(j, h, lambda copy: copy.wait())
+            which, slot = table[at + 1 + 2 * h], table[at + 2 + 2 * h]
+            for w, out in enumerate(outs):
+
+                @pl.when(which == w)
+                def _(out=out, slot=slot, total=total, h=h):
+                    for z in range(NZ):
+                        for c in range(2):
+                            row = c * 256 + z * 32 + h * 16
+                            to = z * 32 + c * 16
+                            out[slot, to : to + 16, :] = total[row : row + 16, :]
 
 
 def gradient_shapes(near, low):
     half, width = near.shape
     cols = width // 8
     slots = jax.ShapeDtypeStruct((2, cols // 2, low), jnp.bfloat16)
-    scratch = [
-        ((2 * half, low), jnp.bfloat16),
-        ((4, 2, cols // 2, low), jnp.bfloat16),
-    ]
-    return slots, scratch
-
-
-def finish(table, own, other, pieces, before, near, far):
+    return slots
+
+
+def finish(table, own, other, pieces, parts, near, far):
     half, width = own.shape
     n, depth, low = len(pieces), pieces[0].shape[0], pieces[0].shape[1] // 2
-    slots, scratch = gradient_shapes(near, low)
+    slots = gradient_shapes(near, low)
 
     def kernel(table, own, other, *refs):
-        pieces, (before, near, far, out) = refs[:n], refs[n : n + 4]
-        outs, (blocks, basis, projected, dealt, sems) = refs[n + 4 : -5], refs[-5:]
-        copies = Copies(sems.at[pl.ds(8, 3 * n + 2)])
-        started = fetch_pieces(copies, table, 2, own, other, pieces, blocks, basis)
+        pieces, (one, two, near, far, projected) = refs[:n], refs[n : n + 5]
+        outs, (blocks, basis, sems) = refs[n + 5 : -3], refs[-3:]
+        copies = Copies(sems)
+        started = fetch_pieces(copies, table, 2, own, other, pieces, blocks)
+        lanes = pl.ds(pl.multiple_of(table[CORE] * low, low), low)
+        for j, piece in enumerate(pieces):
+            basis[j * depth : (j + 1) * depth, :] = piece[:, lanes]
         wait(started)
         for m in range(4):
             rows = pl.ds(m * half // 2, half // 2)
             part = dot(blocks[rows, :], basis[...], ((1,), (0,)))
-            projected[rows, :] = (before[rows, :] + part).astype(projected.dtype)
-        kept = copies(projected, out)
-        write_tiles(sems, table, 0, near, far, projected, dealt, outs)
-        kept.wait()
+            part += one[rows, :] + two[rows, :]
+            projected[rows, :] = part.astype(projected.dtype)
+        write_tiles(table, 0, near, far, projected, outs)
 
     return run(
         kernel,
         table,
-        (own, other, *pieces, before, near, far),
+        (own, other, *pieces, *parts, near, far),
         [jax.ShapeDtypeStruct((2 * half, low), jnp.bfloat16)] + [slots] * 4,
         [
             ((2 * half, n * depth), jnp.bfloat16),
             ((n * depth, low), jnp.bfloat16),
-            *scratch,
         ],
-        3 * n + 10,
+        2 * n,
         2 * half * width * low,
         11 * 2**20,
-        local=(n + 2, n + 3, n + 4),
+        local=range(2, n + 6),
+        here=True,
         pinned=(0,),
     )
 
@@ -248,55 +234,75 @@
 def gradient(table, near, far, projected):
     half, width = near.shape
     low = projected.shape[1]
-    slots, scratch = gradient_shapes(near, low)
+    slots = gradient_shapes(near, low)
 
     def kernel(table, near, far, source, *refs):
-        outs, (projected, dealt, sems) = refs[:4], refs[4:]
-        Copies(sems.at[pl.ds(8, 1)])(source, projected).wait()
-        write_tiles(sems, table, 1, near, far, projected, dealt, outs)
+        outs = refs[:4]
+        write_tiles(table, 1, near, far, source, outs)
 
     return run(
         kernel,
         table,
         (near, far, projected),
         [slots] * 4,
-        scratch,
-        9,
+        [],
+        1,
         2 * half * width * low,
         7 * 2**20,
-        local=(0, 1),
-    )
-
-
-def expand(table, mine, rest, update, weight):
+        local=(0, 1, 2),
+        here=True,
+    )
+
+
+def assemble(table, mine, rest):
     depth, low_rank = mine[0].shape
-    cols = weight.shape[1]
     n = len(mine)
 
     def kernel(table, *refs):
-        pieces, (factor, weight, out, new, sems) = refs[: 2 * n], refs[2 * n :]
-        copies = Copies(sems)
-        ended = []
+        out, sems = refs[2 * n :]
+        copies, started = Copies(sems), []
         for j in range(n):
             for i, side in ((j, table[CORE]), (n + j, 1 - table[CORE])):
                 at = pl.multiple_of((2 * table[SHARDS + j] + side) * depth, depth)
-                rows = pl.ds(at, depth)
-                total = dot(pieces[i][...], factor[...], ((1,), (1,)))
-                new[i] = (weight[rows, :].astype(jnp.float32) - rate * total).astype(new.dtype)
-                ended.append(copies(new.at[i], out.at[rows, :]))
+                started.append(copies(refs[i], out.at[pl.ds(at, depth), :]))
+        wait(started)
+
+    return run(
+        kernel,
+        table,
+        (*mine, *rest),
+        [jax.ShapeDtypeStruct((2 * n * depth, low_rank), jnp.bfloat16)],
+        [],
+        2 * n,
+        0,
+        16 * 2**20,
+        here=True,
+    )[0]
+
+
+def expand(table, rows, update, weight):
+    parts = 4
+    size, cols = weight.shape[0] // parts, weight.shape[1]
+
+    def kernel(table, rows, update, weight, out, new, sems):
+        copies, ended = Copies(sems), []
+        for i in range(parts):
+            at = pl.ds(i * size, size)
+            total = dot(rows[at, :], update[...], ((1,), (1,)))
+            new[i] = (weight[at, :].astype(jnp.float32) - rate * total).astype(new.dtype)
+            ended.append(copies(new.at[i], out.at[at, :]))
         wait(ended)
 
-    args = (*mine, *rest, update, weight)
     return run(
         kernel,
         table,
-        args,
+        (rows, update, weight),
         [jax.ShapeDtypeStruct(weight.shape, weight.dtype)],
-        [((2 * n, depth, cols), jnp.bfloat16)],
-        2 * n,
-        2 * weight.size * low_rank,
+        [((parts, size, cols), jnp.bfloat16)],
+        parts,
+        2 * weight.size * rows.shape[1],
         13 * 2**20,
-        local=range(len(args)),
+        local=range(3),
     )[0]
 
 
@@ -322,8 +328,8 @@
 
 
 TURNED = [4 * (j // 4) + (4 - j) % 4 for j in range(8)]
-PHASES = ((0, 1, 4), (2, 5, 3, 6), (7,))
-CORE, SHARDS, TILES, PIECES = 0, 1, (9, 29), (49, 55, 63)
+ORDER = (0, 8, 1, 9, 4, 12, 2, 10, 5, 13, 3, 6, 11, 14, 7, 15)
+CORE, SHARDS, TILES, PIECES = 0, 1, (9, 29), (49, 55, 61)
 
 
 def device_row(x, y, core):
@@ -331,9 +337,11 @@
     row = [core] + shards
     for call in range(2):
         row += tile_rows(core, x, y, call)
-    for phase in PHASES:
-        for j in phase:
-            row += [2 * shards[j] + core, 2 * shards[TURNED[j]] + 1 - core]
+    for j in ORDER:
+        if j < 8:
+            row.append(2 * shards[j] + core)
+        else:
+            row.append(2 * shards[TURNED[j - 8]] + 1 - core)
     return row
 
 
@@ -356,17 +364,17 @@
         swap(y0), swap(x1), ring_y(x1), ring_x(x1), x1, y0
     )
     both = (activations, other_activations)
-    begun = project(table, 0, *both, [basis, s_x0, x1, s_x1, y0, s_y0], vmem=LARGE)
-    s_y1, s_x2, y2, x3, begun, x2, y1, cotangent = together(
-        swap(y1), swap(x2), ring_y(x2), ring_x(x2), begun, x2, y1, cotangent
-    )
-    cotangent, s_x3, s_y2 = together(cotangent, swap(x3), swap(y2))
-    other_cotangent = swap(cotangent)
-    begun = project(table, 1, *both, [x2, s_x2, y1, s_y1, x3, s_x3, y2, s_y2], begun, SMALL)
-    other_cotangent, y3, begun = together(other_cotangent, ring_y(x3), begun)
+    early = project(table, 0, *both, [basis, s_x0, x1, s_x1, y0, s_y0], LARGE)
+    s_y1, s_x2, y2, x3, early, x2, y1, cotangent = together(
+        swap(y1), swap(x2), ring_y(x2), ring_x(x2), early, x2, y1, cotangent
+    )
+    late = project(table, 1, *both, [x2, s_x2, y1, s_y1, x3, y2])
+    other_cotangent, s_x3, s_y2, y3, late, x3, y2 = together(
+        swap(cotangent), swap(x3), swap(y2), ring_y(x3), late, x3, y2
+    )
     s_y3 = swap(y3)
     projected, *opposite_own = finish(
-        table, *both, (y3, s_y3), begun, cotangent, other_cotangent
+        table, *both, (s_x3, s_y2, y3, s_y3), (early, late), cotangent, other_cotangent
     )
     mine = (basis, x1, x2, x3, y0, y1, y2, y3)
     rest = (s_x0, s_x1, s_x2, s_x3, s_y0, s_y1, s_y2, s_y3)
@@ -383,6 +391,8 @@
         for terms in ((own_a, next_a, last_a), (own_b, next_b, last_b))
         for i in range(2)
     ]
+    rows = assemble(table, mine, rest)
+    rows, own = together(rows, own)
     terms = added(
         own,
         along(opposite, 2, False),
@@ -400,7 +410,7 @@
     copies = jnp.broadcast_to(update[None], (16, owned, low_rank))
     update = lax.all_to_all(copies, "dp", 0, 0, tiled=True).reshape(16 * owned, low_rank)
 
-    new_weight = expand(table, mine, rest, update, weight)
+    new_weight = expand(table, rows, update, weight)
     return (new_weight, moment_one.T.reshape(first.shape), moment_two.T.reshape(first.shape))
 
 

time: 143 us -> 141 us (0.986)
  waiting for transfers between devices: 37.7 us -> 33.6 us
  Pallas kernels: 26.1 us -> 28 us
  starting transfers between devices: 28.5 us -> 30.2 us
  local copies, waits for them, and re-layouts: 2.92 us -> 1.34 us
    ppermute x26, waiting for transfers between devices: 37.7 us -> 33.6 us  [route(): return lax.ppermute(value, AXES, sorted(pairs))]
    pallas_call x5 -> x6, Pallas kernels: 26.1 us -> 28 us  [run(): pl.pallas_call(kernel, grid_spec=pltpu.PrefetchScalarGridSpec(num_scalar_...]
    ppermute x26, starting transfers between devices: 28.5 us -> 30.2 us  [route(): return lax.ppermute(value, AXES, sorted(pairs))]
    unnamed x36, local copies, waits for them, and re-layouts: 1.66 us -> 0.08 us
  transfers between devices with their start and end apart: 26 -> 26, of which waited for: 14 -> 12; matrix products, arithmetic and copies ran while one was open for 1% -> 1% of each run, Pallas kernels for 11% -> 13%
where the time goes in v1:
time: 141 us
  blocking collectives  44.9 us (32%)
  waiting for transfers between devices  33.6 us (24%)
  starting transfers between devices  30.2 us (21%)
  Pallas kernels  28 us (20%)
  other arithmetic  1.54 us (1%)
    ppermute x26, waiting for transfers between devices, route(): return lax.ppermute(value, AXES, sorted(pairs))  33.6 us
    ppermute x26, starting transfers between devices, route(): return lax.ppermute(value, AXES, sorted(pairs))  30.2 us
    pallas_call x6, Pallas kernels, run(): pl.pallas_call(kernel, grid_spec=pltpu.PrefetchScalarGridSpec(num_scalar_...  28 us
    all_to_all x1, blocking collectives, body(): lax.all_to_all(copies, 'dp', 0, 0, tiled=True).reshape(16 * owned, low_rank)  25.4 us
    all_to_all x1, blocking collectives, exchange(): lax.all_to_all(value, AXES, 0, 0, tiled=True, axis_index_groups=groups)  19.5 us
  transfers between devices with their start and end apart: 26, of which 12 were waited for; matrix products, arithmetic and copies ran while one was open for 1% of the time, Pallas kernels for 13%

profile of v1, /device:TPU:8, one launch (start us, length us, event | category | flops | bytes accessed | tf_op | source)
XLA Modules:
  0.0 140.7 jit_solution(1346731565993010957)
XLA Ops:
  0.6 0.1 collective-permute-start
  0.7 1.6 %collective-permute-start.3 = (bf16[256,1024]{1,0:T(8,128)(2,1)}, bf16[256,1024]{1,0:T(8,128)(2,1)S(1)}, u32[]{:S(2)}, u32[]{:S(2)}) collective-permute-start(bf16[256,1024]{1,0:T(8,128)(2,1)} %refs_0_.3), channel_id=1, source_target_pairs={{0,2},{1,7},{2,4},{3,1},{4,6},{5,3},{6,0},{7,5},{8,10},{9,15},{10,... | collective-permute-start | bytes 1572872 | tf_op jit(solution)/shard_map/ppermute | solution.py:36
  2.3 1.6 %collective-permute-start.2 = (bf16[256,1024]{1,0:T(8,128)(2,1)}, bf16[256,1024]{1,0:T(8,128)(2,1)S(1)}, u32[]{:S(2)}, u32[]{:S(2)}) collective-permute-start(bf16[256,1024]{1,0:T(8,128)(2,1)} %refs_0_.3), channel_id=1, source_target_pairs={{0,8},{1,25},{2,10},{3,27},{4,12},{5,29},{6,14},{7,31},{8,16},{9,1... | collective-permute-start | bytes 1572872 | tf_op jit(solution)/shard_map/ppermute | solution.py:36
  3.9 7.5 %collective-permute-done.3.refs_2_.refs_1_ = bf16[256,1024]{1,0:T(8,128)(2,1)S(1)} collective-permute-done((bf16[256,1024]{1,0:T(8,128)(2,1)}, bf16[256,1024]{1,0:T(8,128)(2,1)S(1)}, u32[]{:S(2)}, u32[]{:S(2)}) %collective-permute-start.3) | collective-permute-done | bytes 524320 | tf_op jit(solution)/shard_map/ppermute | solution.py:36
  11.4 0.3 collective-permute-done.2.refs_4_
  11.7 0.3 collective-permute-start.4
  12.0 1.3 collective-permute-start.7
  13.4 1.6 %collective-permute-start.6 = (bf16[256,1024]{1,0:T(8,128)(2,1)S(1)}, bf16[256,1024]{1,0:T(8,128)(2,1)S(1)}, u32[]{:S(2)}, u32[]{:S(2)}) collective-permute-start(bf16[256,1024]{1,0:T(8,128)(2,1)S(1)} %collective-permute-done.3.refs_2_.refs_1_), channel_id=1, source_target_pairs={{0,8},{1,25},{2,10},{3,27},{4,12},{5,29},{6,14},{7,31},{8,16},{9,1... | collective-permute-start | bytes 1572872 | tf_op jit(solution)/shard_map/ppermute | solution.py:36
  15.0 1.9 %collective-permute-start.5 = (bf16[256,1024]{1,0:T(8,128)(2,1)S(1)}, bf16[256,1024]{1,0:T(8,128)(2,1)S(1)}, u32[]{:S(2)}, u32[]{:S(2)}) collective-permute-start(bf16[256,1024]{1,0:T(8,128)(2,1)S(1)} %collective-permute-done.3.refs_2_.refs_1_), channel_id=1, source_target_pairs={{0,1},{1,0},{2,3},{3,2},{4,5},{5,4},{6,7},{7,6},{8,9},{9,8},{10,11... | collective-permute-start | bytes 1572872 | tf_op jit(solution)/shard_map/ppermute | solution.py:36
  16.9 5.5 %collective-permute-done.7.refs_0_.refs_2_ = bf16[256,1024]{1,0:T(8,128)(2,1)S(1)} collective-permute-done((bf16[256,1024]{1,0:T(8,128)(2,1)S(1)}, bf16[256,1024]{1,0:T(8,128)(2,1)S(1)}, u32[]{:S(2)}, u32[]{:S(2)}) %collective-permute-start.7) | collective-permute-done | bytes 524320 | tf_op jit(solution)/shard_map/ppermute | solution.py:36
  22.4 0.1 collective-permute-done.6.refs_2_.refs_5_
  22.6 0.5 collective-permute-start.8
  23.0 0.8 collective-permute-start.11
  23.8 1.6 %collective-permute-start.10 = (bf16[256,1024]{1,0:T(8,128)(2,1)S(1)}, bf16[256,1024]{1,0:T(8,128)(2,1)}, u32[]{:S(2)}, u32[]{:S(2)}) collective-permute-start(bf16[256,1024]{1,0:T(8,128)(2,1)S(1)} %collective-permute-done.7.refs_0_.refs_2_), channel_id=1, source_target_pairs={{0,8},{1,25},{2,10},{3,27},{4,12},{5,29},{6,14},{7,31},{8,16},{9,1... | collective-permute-start | bytes 1572872 | tf_op jit(solution)/shard_map/ppermute | solution.py:36
  25.4 2.0 %collective-permute-start.9 = (bf16[256,1024]{1,0:T(8,128)(2,1)S(1)}, bf16[256,1024]{1,0:T(8,128)(2,1)}, u32[]{:S(2)}, u32[]{:S(2)}) collective-permute-start(bf16[256,1024]{1,0:T(8,128)(2,1)S(1)} %collective-permute-done.7.refs_0_.refs_2_), channel_id=1, source_target_pairs={{0,1},{1,0},{2,3},{3,2},{4,5},{5,4},{6,7},{7,6},{8,9},{9,8},{10,11... | collective-permute-start | bytes 1572872 | tf_op jit(solution)/shard_map/ppermute | solution.py:36
  27.5 1.2 dynamic-slice_bitcast_fusion.table
  28.7 6.3 %shard_map.94.refs_4_ = f32[1024,512]{1,0:T(8,128)} custom-call(s32[65]{0:T(128)} %dynamic-slice_bitcast_fusion.table, bf16[512,4096]{1,0:T(8,128)(2,1)} %own.5, bf16[512,4096]{1,0:T(8,128)(2,1)} %collective-permute-done.other, bf16[256,1024]{1,0:T(8,128)(2,1)} %refs_0_.3, bf16[256,1024]{1,0:T(8,128)(2,1)} %copy-done.9, bf16[256,1024]{1,0:T(8,128)(2,1)} %copy-done.5, ...), custom_call_target="tpu_custom_call" | custom-call | flops 1610612736 | bytes 6291456 | tf_op jit(solution)/shard_map/pallas_call | solution.py:85
  35.2 0.5 collective-permute-start.14
  35.7 1.8 %collective-permute-start.13 = (bf16[256,1024]{1,0:T(8,128)(2,1)}, bf16[256,1024]{1,0:T(8,128)(2,1)S(1)}, u32[]{:S(2)}, u32[]{:S(2)}) collective-permute-start(bf16[256,1024]{1,0:T(8,128)(2,1)} %collective-permute-done.11.refs_4_.refs_3_), channel_id=1, source_target_pairs={{0,1},{1,0},{2,3},{3,2},{4,5},{5,4},{6,7},{7,6},{8,9},{9,8},{10,11... | collective-permute-start | bytes 1572872 | tf_op jit(solution)/shard_map/ppermute | solution.py:36
  37.5 4.9 %shard_map.95.refs_5_ = f32[1024,512]{1,0:T(8,128)S(1)} custom-call(s32[65]{0:T(128)S(1)} %copy-done.15, bf16[512,4096]{1,0:T(8,128)(2,1)S(1)} %copy-done, bf16[512,4096]{1,0:T(8,128)(2,1)} %collective-permute-done.other, bf16[256,1024]{1,0:T(8,128)(2,1)S(1)} %collective-permute-done.7.refs_0_.refs_2_, ...), custom_call_target="tpu_custom_call" | custom-call | flops 1610612736 | bytes 6291456 | tf_op jit(solution)/shard_map/pallas_call | solution.py:85
  42.4 0.9 collective-permute-done.14.refs_14_.refs_1_
  43.3 1.8 %collective-permute-done.15.refs_7_.refs_2_ = bf16[256,1024]{1,0:T(8,128)(2,1)S(1)} collective-permute-done((bf16[256,1024]{1,0:T(8,128)(2,1)}, bf16[256,1024]{1,0:T(8,128)(2,1)S(1)}, u32[]{:S(2)}, u32[]{:S(2)}) %collective-permute-start.15) | collective-permute-done | bytes 524320 | tf_op jit(solution)/shard_map/ppermute | solution.py:36
  45.1 1.9 %collective-permute-done.16.refs_13_.refs_3_ = bf16[256,1024]{1,0:T(8,128)(2,1)S(1)} collective-permute-done((bf16[256,1024]{1,0:T(8,128)(2,1)S(1)}, bf16[256,1024]{1,0:T(8,128)(2,1)S(1)}, u32[]{:S(2)}, u32[]{:S(2)}) %collective-permute-start.16) | collective-permute-done | bytes 524320 | tf_op jit(solution)/shard_map/ppermute | solution.py:36
  47.0 6.4 %shard_map.97 = (bf16[1024,512]{1,0:T(8,128)(2,1)S(1)}, bf16[2,256,512]{2,1,0:T(8,128)(2,1)S(1)}, bf16[2,256,512]{2,1,0:T(8,128)(2,1)S(1)}, bf16[2,256,512]{2,1,0:T(8,128)(2,1)S(1)}, bf16[2,256,512]{2,1,0:T(8,128)(2,1)S(1)}) custom-call(s32[65]{0:T(128)S(1)} %copy-done.15, bf16[512,4096]{1,0:T(8,128)(2,1)S(1)} %copy-done, ...), custom_call_target="tpu_custom_call" | custom-call | flops 2147483648 | bytes 11534336 | tf_op jit(solution)/shard_map/pallas_call | solution.py:85
  53.4 2.3 %collective-permute-start.17 = (bf16[2,256,512]{2,1,0:T(8,128)(2,1)S(1)}, bf16[2,256,512]{2,1,0:T(8,128)(2,1)S(1)}, u32[]{:S(2)}, u32[]{:S(2)}) collective-permute-start(bf16[2,256,512]{2,1,0:T(8,128)(2,1)S(1)} %get-tuple-element.67), channel_id=1, source_target_pairs={{0,2},{1,9},{2,4},{3,11},{4,6},{5,13},{6,0},{7,15},{8,10},{9,17},{... | collective-permute-start | bytes 1572872 | tf_op jit(solution)/shard_map/ppermute | solution.py:36
  55.7 1.0 collective-permute-start.21
  56.7 3.9 %shard_map.98 = (bf16[2,256,512]{2,1,0:T(8,128)(2,1)S(1)}, bf16[2,256,512]{2,1,0:T(8,128)(2,1)S(1)}, bf16[2,256,512]{2,1,0:T(8,128)(2,1)S(1)}, bf16[2,256,512]{2,1,0:T(8,128)(2,1)S(1)}) custom-call(s32[65]{0:T(128)S(1)} %copy-done.15, bf16[512,4096]{1,0:T(8,128)(2,1)S(1)} %copy-done.1, bf16[512,4096]{1,0:T(8,128)(2,1)S(1)} %collective-permute-done.12.refs_7_.far, ...), custom_call_target="tpu_custom_call" | custom-call | flops 2147483648 | bytes 7340032 | tf_op jit(solution)/shard_map/pallas_call | solution.py:85
  60.7 0.9 collective-permute-start.19
  61.6 1.2 collective-permute-start.20
  62.8 1.1 collective-permute-done.17
  63.9 0.1 add_convert_fusion.1
  64.0 1.3 collective-permute-start.18
  65.3 0.1 add_convert_fusion
  65.5 2.3 %collective-permute-start.22 = (bf16[2,256,512]{2,1,0:T(8,128)(2,1)S(1)}, bf16[2,256,512]{2,1,0:T(8,128)(2,1)S(1)}, u32[]{:S(2)}, u32[]{:S(2)}) collective-permute-start(bf16[2,256,512]{2,1,0:T(8,128)(2,1)S(1)} %add_convert_fusion), channel_id=1, source_target_pairs={{0,6},{1,25},{2,0},{3,27},{4,2},{5,29},{6,4},{7,31},{8,14},{9,1},{... | collective-permute-start | bytes 1572872 | tf_op jit(solution)/shard_map/ppermute | solution.py:36
  67.8 2.7 %collective-permute-done.19 = bf16[2,256,512]{2,1,0:T(8,128)(2,1)S(1)} collective-permute-done((bf16[2,256,512]{2,1,0:T(8,128)(2,1)S(1)}, bf16[2,256,512]{2,1,0:T(8,128)(2,1)S(1)}, u32[]{:S(2)}, u32[]{:S(2)}) %collective-permute-start.19) | collective-permute-done | bytes 524320 | tf_op jit(solution)/shard_map/ppermute | solution.py:36
  70.5 7.1 %collective-permute-done.18 = bf16[2,256,512]{2,1,0:T(8,128)(2,1)S(1)} collective-permute-done((bf16[2,256,512]{2,1,0:T(8,128)(2,1)S(1)}, bf16[2,256,512]{2,1,0:T(8,128)(2,1)S(1)}, u32[]{:S(2)}, u32[]{:S(2)}) %collective-permute-start.18) | collective-permute-done | bytes 524320 | tf_op jit(solution)/shard_map/ppermute | solution.py:36
  77.6 0.2 fusion.2
  77.8 0.6 collective-permute-start.24
  78.4 0.2 fusion.1
  78.6 4.9 %collective-permute-start.23 = (bf16[256,512]{1,0:T(8,128)(2,1)S(1)}, bf16[256,512]{1,0:T(8,128)(2,1)S(1)}, u32[]{:S(2)}, u32[]{:S(2)}) collective-permute-start(bf16[256,512]{1,0:T(8,128)(2,1)S(1)} %get-tuple-element.75), channel_id=1, source_target_pairs={{0,16},{1,5},{2,18},{3,7},{4,20},{5,1},{6,22},{7,3},{8,24},{9,13},... | collective-permute-start | bytes 786440 | tf_op jit(solution)/shard_map/ppermute | solution.py:36
  83.6 2.5 %shard_map.96.rows = bf16[4096,1024]{1,0:T(8,128)(2,1)S(1)} custom-call(s32[65]{0:T(128)S(1)} %copy-done.15, bf16[256,1024]{1,0:T(8,128)(2,1)S(1)} %copy-done.4, bf16[256,1024]{1,0:T(8,128)(2,1)S(1)} %copy-done.6, bf16[256,1024]{1,0:T(8,128)(2,1)S(1)} %collective-permute-done.7.refs_0_.refs_2_, bf16[256,1024]{1,0:T(8,128)(2,1)} %collective-permute-done.11.refs_4_.refs_3_, ...), custom_call_target="tpu_custom_call" | custom-call | bytes 16777216 | tf_op jit(solution)/shard_map/pallas_call | solution.py:85
  86.1 1.8 %collective-permute-done.23 = bf16[256,512]{1,0:T(8,128)(2,1)S(1)} collective-permute-done((bf16[256,512]{1,0:T(8,128)(2,1)S(1)}, bf16[256,512]{1,0:T(8,128)(2,1)S(1)}, u32[]{:S(2)}, u32[]{:S(2)}) %collective-permute-start.23) | collective-permute-done | bytes 262176 | tf_op jit(solution)/shard_map/ppermute | solution.py:36
  88.0 2.7 %collective-permute-done.25 = bf16[256,512]{1,0:T(8,128)(2,1)S(1)} collective-permute-done((bf16[256,512]{1,0:T(8,128)(2,1)S(1)}, bf16[256,512]{1,0:T(8,128)(2,1)S(1)}, u32[]{:S(2)}, u32[]{:S(2)}) %collective-permute-start.25) | collective-permute-done | bytes 262176 | tf_op jit(solution)/shard_map/ppermute | solution.py:36
  90.7 0.1 add_convert_fusion.2
  90.8 19.5 %all_to_all.10 = bf16[16,16,512]{2,1,0:T(8,128)(2,1)S(1)} all-to-all(bf16[16,16,512]{2,1,0:T(8,128)(2,1)S(1)} %bitcast.42), channel_id=1, replica_groups={{0,1,32,33,64,65,96,97,128,129,160,161,192,193,224,225},{2,3,34,35,66,6..., dimensions={0} | all-to-all | bytes 524288 | tf_op jit(solution)/shard_map/all_to_all | solution.py:71
  110.4 0.7 fusion.6
  111.2 25.4 %all_to_all.11 = bf16[16,16,1024]{2,1,0:T(8,128)(2,1)S(1)} all-to-all(bf16[16,16,1024]{2,1,0:T(8,128)(2,1)S(1)} %broadcast_in_dim.2), channel_id=1, replica_groups=mesh['dp'=16,'fsdp'=16] {'dp'}, dimensions={0} | all-to-all | bytes 1048576 | tf_op jit(solution)/shard_map/all_to_all | solution.py:411
  136.6 4.0 %shard_map.99 = bf16[4096,256]{1,0:T(8,128)(2,1)} custom-call(s32[65]{0:T(128)S(1)} %copy-done.15, bf16[4096,1024]{1,0:T(8,128)(2,1)S(1)} %shard_map.96.rows, bf16[256,1024]{1,0:T(8,128)(2,1)S(1)} %bitcast.41, bf16[4096,256]{1,0:T(8,128)(2,1)S(1)} %copy-done.3), custom_call_target="tpu_custom_call" | custom-call | flops 2147483648 | bytes 13631488 | tf_op jit(solution)/shard_map/pallas_call | solution.py:85
  (58 shorter events, 0.3 us)
Async XLA Ops:
  0.6 11.1 %collective-permute-start = (bf16[512,4096]{1,0:T(8,128)(2,1)}, bf16[512,4096]{1,0:T(8,128)(2,1)}, u32[]{:S(2)}, u32[]{:S(2)}) collective-permute-start(bf16[512,4096]{1,0:T(8,128)(2,1)} %own.5), channel_id=1, source_target_pairs={{0,1},{1,0},{2,3},{3,2},{4,5},{5,4},{6,7},{7,6},{8,9},{9,8},{10,11... | collective-permute-start | bytes 12582920 | tf_op jit(solution)/shard_map/ppermute | solution.py:36
  0.7 10.7 %collective-permute-start.3 = (bf16[256,1024]{1,0:T(8,128)(2,1)}, bf16[256,1024]{1,0:T(8,128)(2,1)S(1)}, u32[]{:S(2)}, u32[]{:S(2)}) collective-permute-start(bf16[256,1024]{1,0:T(8,128)(2,1)} %refs_0_.3), channel_id=1, source_target_pairs={{0,2},{1,7},{2,4},{3,1},{4,6},{5,3},{6,0},{7,5},{8,10},{9,15},{10,... | collective-permute-start | bytes 1572872 | tf_op jit(solution)/shard_map/ppermute | solution.py:36
  2.3 9.4 %collective-permute-start.2 = (bf16[256,1024]{1,0:T(8,128)(2,1)}, bf16[256,1024]{1,0:T(8,128)(2,1)S(1)}, u32[]{:S(2)}, u32[]{:S(2)}) collective-permute-start(bf16[256,1024]{1,0:T(8,128)(2,1)} %refs_0_.3), channel_id=1, source_target_pairs={{0,8},{1,25},{2,10},{3,27},{4,12},{5,29},{6,14},{7,31},{8,16},{9,1... | collective-permute-start | bytes 1572872 | tf_op jit(solution)/shard_map/ppermute | solution.py:36
  3.9 7.8 %collective-permute-start.1 = (bf16[256,1024]{1,0:T(8,128)(2,1)}, bf16[256,1024]{1,0:T(8,128)(2,1)S(1)}, u32[]{:S(2)}, u32[]{:S(2)}) collective-permute-start(bf16[256,1024]{1,0:T(8,128)(2,1)} %refs_0_.3), channel_id=1, source_target_pairs={{0,1},{1,0},{2,3},{3,2},{4,5},{5,4},{6,7},{7,6},{8,9},{9,8},{10,11... | collective-permute-start | bytes 1572872 | tf_op jit(solution)/shard_map/ppermute | solution.py:36
  11.4 17.3 %copy-start.5 = (bf16[256,1024]{1,0:T(8,128)(2,1)}, bf16[256,1024]{1,0:T(8,128)(2,1)S(1)}, u32[]{:S(2)}) copy-start(bf16[256,1024]{1,0:T(8,128)(2,1)S(1)} %collective-permute-done.3.refs_2_.refs_1_) | copy-start | bytes 1572868
  11.7 17.0 %copy-start.7 = (bf16[256,1024]{1,0:T(8,128)(2,1)}, bf16[256,1024]{1,0:T(8,128)(2,1)S(1)}, u32[]{:S(2)}) copy-start(bf16[256,1024]{1,0:T(8,128)(2,1)S(1)} %collective-permute-done.2.refs_4_) | copy-start | bytes 1572868
  11.7 17.0 %copy-start.9 = (bf16[256,1024]{1,0:T(8,128)(2,1)}, bf16[256,1024]{1,0:T(8,128)(2,1)S(1)}, u32[]{:S(2)}) copy-start(bf16[256,1024]{1,0:T(8,128)(2,1)S(1)} %collective-permute-done.1.refs_1_.refs_8_) | copy-start | bytes 1572868
  11.7 5.2 %collective-permute-start.4 = (bf16[256,1024]{1,0:T(8,128)(2,1)S(1)}, bf16[256,1024]{1,0:T(8,128)(2,1)S(1)}, u32[]{:S(2)}, u32[]{:S(2)}) collective-permute-start(bf16[256,1024]{1,0:T(8,128)(2,1)S(1)} %collective-permute-done.2.refs_4_), channel_id=1, source_target_pairs={{0,1},{1,0},{2,3},{3,2},{4,5},{5,4},{6,7},{7,6},{8,9},{9,8},{10,11... | collective-permute-start | bytes 1572872 | tf_op jit(solution)/shard_map/ppermute | solution.py:36
  12.0 10.4 %collective-permute-start.7 = (bf16[256,1024]{1,0:T(8,128)(2,1)S(1)}, bf16[256,1024]{1,0:T(8,128)(2,1)S(1)}, u32[]{:S(2)}, u32[]{:S(2)}) collective-permute-start(bf16[256,1024]{1,0:T(8,128)(2,1)S(1)} %collective-permute-done.3.refs_2_.refs_1_), channel_id=1, source_target_pairs={{0,2},{1,7},{2,4},{3,1},{4,6},{5,3},{6,0},{7,5},{8,10},{9,15},{10,... | collective-permute-start | bytes 1572872 | tf_op jit(solution)/shard_map/ppermute | solution.py:36
  13.4 9.2 %collective-permute-start.6 = (bf16[256,1024]{1,0:T(8,128)(2,1)S(1)}, bf16[256,1024]{1,0:T(8,128)(2,1)S(1)}, u32[]{:S(2)}, u32[]{:S(2)}) collective-permute-start(bf16[256,1024]{1,0:T(8,128)(2,1)S(1)} %collective-permute-done.3.refs_2_.refs_1_), channel_id=1, source_target_pairs={{0,8},{1,25},{2,10},{3,27},{4,12},{5,29},{6,14},{7,31},{8,16},{9,1... | collective-permute-start | bytes 1572872 | tf_op jit(solution)/shard_map/ppermute | solution.py:36
  15.0 7.6 %collective-permute-start.5 = (bf16[256,1024]{1,0:T(8,128)(2,1)S(1)}, bf16[256,1024]{1,0:T(8,128)(2,1)S(1)}, u32[]{:S(2)}, u32[]{:S(2)}) collective-permute-start(bf16[256,1024]{1,0:T(8,128)(2,1)S(1)} %collective-permute-done.3.refs_2_.refs_1_), channel_id=1, source_target_pairs={{0,1},{1,0},{2,3},{3,2},{4,5},{5,4},{6,7},{7,6},{8,9},{9,8},{10,11... | collective-permute-start | bytes 1572872 | tf_op jit(solution)/shard_map/ppermute | solution.py:36
  16.9 11.8 %copy-start.11 = (bf16[256,1024]{1,0:T(8,128)(2,1)}, bf16[256,1024]{1,0:T(8,128)(2,1)S(1)}, u32[]{:S(2)}) copy-start(bf16[256,1024]{1,0:T(8,128)(2,1)S(1)} %collective-permute-done.4.refs_5_.refs_12_) | copy-start | bytes 1572868
  22.6 1.3 copy-start.13
  22.6 12.5 %collective-permute-start.8 = (bf16[256,1024]{1,0:T(8,128)(2,1)S(1)}, bf16[256,1024]{1,0:T(8,128)(2,1)}, u32[]{:S(2)}, u32[]{:S(2)}) collective-permute-start(bf16[256,1024]{1,0:T(8,128)(2,1)S(1)} %collective-permute-done.6.refs_2_.refs_5_), channel_id=1, source_target_pairs={{0,1},{1,0},{2,3},{3,2},{4,5},{5,4},{6,7},{7,6},{8,9},{9,8},{10,11... | collective-permute-start | bytes 1572872 | tf_op jit(solution)/shard_map/ppermute | solution.py:36
  23.0 12.1 %collective-permute-start.11 = (bf16[256,1024]{1,0:T(8,128)(2,1)S(1)}, bf16[256,1024]{1,0:T(8,128)(2,1)}, u32[]{:S(2)}, u32[]{:S(2)}) collective-permute-start(bf16[256,1024]{1,0:T(8,128)(2,1)S(1)} %collective-permute-done.7.refs_0_.refs_2_), channel_id=1, source_target_pairs={{0,2},{1,7},{2,4},{3,1},{4,6},{5,3},{6,0},{7,5},{8,10},{9,15},{10,... | collective-permute-start | bytes 1572872 | tf_op jit(solution)/shard_map/ppermute | solution.py:36
  23.8 11.2 %collective-permute-start.10 = (bf16[256,1024]{1,0:T(8,128)(2,1)S(1)}, bf16[256,1024]{1,0:T(8,128)(2,1)}, u32[]{:S(2)}, u32[]{:S(2)}) collective-permute-start(bf16[256,1024]{1,0:T(8,128)(2,1)S(1)} %collective-permute-done.7.refs_0_.refs_2_), channel_id=1, source_target_pairs={{0,8},{1,25},{2,10},{3,27},{4,12},{5,29},{6,14},{7,31},{8,16},{9,1... | collective-permute-start | bytes 1572872 | tf_op jit(solution)/shard_map/ppermute | solution.py:36
  25.4 9.7 %collective-permute-start.9 = (bf16[256,1024]{1,0:T(8,128)(2,1)S(1)}, bf16[256,1024]{1,0:T(8,128)(2,1)}, u32[]{:S(2)}, u32[]{:S(2)}) collective-permute-start(bf16[256,1024]{1,0:T(8,128)(2,1)S(1)} %collective-permute-done.7.refs_0_.refs_2_), channel_id=1, source_target_pairs={{0,1},{1,0},{2,3},{3,2},{4,5},{5,4},{6,7},{7,6},{8,9},{9,8},{10,11... | collective-permute-start | bytes 1572872 | tf_op jit(solution)/shard_map/ppermute | solution.py:36
  28.7 8.8 %copy-start = (bf16[512,4096]{1,0:T(8,128)(2,1)S(1)}, bf16[512,4096]{1,0:T(8,128)(2,1)}, u32[]{:S(2)}) copy-start(bf16[512,4096]{1,0:T(8,128)(2,1)} %own.5) | copy-start | bytes 12582916
  28.7 8.8 %copy-start.15 = (s32[65]{0:T(128)S(1)}, s32[65]{0:T(128)}, u32[]{:S(2)}) copy-start(s32[65]{0:T(128)} %dynamic-slice_bitcast_fusion.table) | copy-start | bytes 784
  35.0 12.0 %copy-start.1 = (bf16[512,4096]{1,0:T(8,128)(2,1)S(1)}, bf16[512,4096]{1,0:T(8,128)(2,1)}, u32[]{:S(2)}) copy-start(bf16[512,4096]{1,0:T(8,128)(2,1)} %near) | copy-start | bytes 12582916
  35.0 12.0 %copy-start.2 = (f32[1024,512]{1,0:T(8,128)S(1)}, f32[1024,512]{1,0:T(8,128)}, u32[]{:S(2)}) copy-start(f32[1024,512]{1,0:T(8,128)} %shard_map.94.refs_4_) | copy-start | bytes 6291460
  35.1 10.0 %collective-permute-start.12 = (bf16[512,4096]{1,0:T(8,128)(2,1)}, bf16[512,4096]{1,0:T(8,128)(2,1)S(1)}, u32[]{:S(2)}, u32[]{:S(2)}) collective-permute-start(bf16[512,4096]{1,0:T(8,128)(2,1)} %near), channel_id=1, source_target_pairs={{0,1},{1,0},{2,3},{3,2},{4,5},{5,4},{6,7},{7,6},{8,9},{9,8},{10,11... | collective-permute-start | bytes 12582920 | tf_op jit(solution)/shard_map/ppermute | solution.py:36
  35.2 8.1 %collective-permute-start.14 = (bf16[256,1024]{1,0:T(8,128)(2,1)}, bf16[256,1024]{1,0:T(8,128)(2,1)S(1)}, u32[]{:S(2)}, u32[]{:S(2)}) collective-permute-start(bf16[256,1024]{1,0:T(8,128)(2,1)} %collective-permute-done.10.refs_5_.refs_6_), channel_id=1, source_target_pairs={{0,1},{1,0},{2,3},{3,2},{4,5},{5,4},{6,7},{7,6},{8,9},{9,8},{10,11... | collective-permute-start | bytes 1572872 | tf_op jit(solution)/shard_map/ppermute | solution.py:36
  35.7 9.4 %collective-permute-start.15 = (bf16[256,1024]{1,0:T(8,128)(2,1)}, bf16[256,1024]{1,0:T(8,128)(2,1)S(1)}, u32[]{:S(2)}, u32[]{:S(2)}) collective-permute-start(bf16[256,1024]{1,0:T(8,128)(2,1)} %collective-permute-done.11.refs_4_.refs_3_), channel_id=1, source_target_pairs={{0,8},{1,25},{2,10},{3,27},{4,12},{5,29},{6,14},{7,31},{8,16},{9,1... | collective-permute-start | bytes 1572872 | tf_op jit(solution)/shard_map/ppermute | solution.py:36
  35.7 9.4 %collective-permute-start.13 = (bf16[256,1024]{1,0:T(8,128)(2,1)}, bf16[256,1024]{1,0:T(8,128)(2,1)S(1)}, u32[]{:S(2)}, u32[]{:S(2)}) collective-permute-start(bf16[256,1024]{1,0:T(8,128)(2,1)} %collective-permute-done.11.refs_4_.refs_3_), channel_id=1, source_target_pairs={{0,1},{1,0},{2,3},{3,2},{4,5},{5,4},{6,7},{7,6},{8,9},{9,8},{10,11... | collective-permute-start | bytes 1572872 | tf_op jit(solution)/shard_map/ppermute | solution.py:36
  45.1 1.9 %collective-permute-start.16 = (bf16[256,1024]{1,0:T(8,128)(2,1)S(1)}, bf16[256,1024]{1,0:T(8,128)(2,1)S(1)}, u32[]{:S(2)}, u32[]{:S(2)}) collective-permute-start(bf16[256,1024]{1,0:T(8,128)(2,1)S(1)} %collective-permute-done.15.refs_7_.refs_2_), channel_id=1, source_target_pairs={{0,1},{1,0},{2,3},{3,2},{4,5},{5,4},{6,7},{7,6},{8,9},{9,8},{10,11... | collective-permute-start | bytes 1572872 | tf_op jit(solution)/shard_map/ppermute | solution.py:36
  53.4 10.5 %collective-permute-start.17 = (bf16[2,256,512]{2,1,0:T(8,128)(2,1)S(1)}, bf16[2,256,512]{2,1,0:T(8,128)(2,1)S(1)}, u32[]{:S(2)}, u32[]{:S(2)}) collective-permute-start(bf16[2,256,512]{2,1,0:T(8,128)(2,1)S(1)} %get-tuple-element.67), channel_id=1, source_target_pairs={{0,2},{1,9},{2,4},{3,11},{4,6},{5,13},{6,0},{7,15},{8,10},{9,17},{... | collective-permute-start | bytes 1572872 | tf_op jit(solution)/shard_map/ppermute | solution.py:36
  55.7 9.6 %collective-permute-start.21 = (bf16[2,256,512]{2,1,0:T(8,128)(2,1)S(1)}, bf16[2,256,512]{2,1,0:T(8,128)(2,1)S(1)}, u32[]{:S(2)}, u32[]{:S(2)}) collective-permute-start(bf16[2,256,512]{2,1,0:T(8,128)(2,1)S(1)} %get-tuple-element.74), channel_id=1, source_target_pairs={{0,6},{1,25},{2,0},{3,27},{4,2},{5,29},{6,4},{7,31},{8,14},{9,1},{... | collective-permute-start | bytes 1572872 | tf_op jit(solution)/shard_map/ppermute | solution.py:36
  60.7 22.9 %copy-start.4 = (bf16[256,1024]{1,0:T(8,128)(2,1)S(1)}, bf16[256,1024]{1,0:T(8,128)(2,1)}, u32[]{:S(2)}) copy-start(bf16[256,1024]{1,0:T(8,128)(2,1)} %refs_0_.3) | copy-start | bytes 1572868
  60.7 22.9 %copy-start.6 = (bf16[256,1024]{1,0:T(8,128)(2,1)S(1)}, bf16[256,1024]{1,0:T(8,128)(2,1)}, u32[]{:S(2)}) copy-start(bf16[256,1024]{1,0:T(8,128)(2,1)} %copy-done.5) | copy-start | bytes 1572868
  60.7 22.9 %copy-start.8 = (bf16[256,1024]{1,0:T(8,128)(2,1)S(1)}, bf16[256,1024]{1,0:T(8,128)(2,1)}, u32[]{:S(2)}) copy-start(bf16[256,1024]{1,0:T(8,128)(2,1)} %copy-done.7) | copy-start | bytes 1572868
  60.7 22.9 %copy-start.10 = (bf16[256,1024]{1,0:T(8,128)(2,1)S(1)}, bf16[256,1024]{1,0:T(8,128)(2,1)}, u32[]{:S(2)}) copy-start(bf16[256,1024]{1,0:T(8,128)(2,1)} %copy-done.9) | copy-start | bytes 1572868
  60.7 22.9 %copy-start.12 = (bf16[256,1024]{1,0:T(8,128)(2,1)S(1)}, bf16[256,1024]{1,0:T(8,128)(2,1)}, u32[]{:S(2)}) copy-start(bf16[256,1024]{1,0:T(8,128)(2,1)} %copy-done.11) | copy-start | bytes 1572868
  60.7 22.9 %copy-start.14 = (bf16[256,1024]{1,0:T(8,128)(2,1)S(1)}, bf16[256,1024]{1,0:T(8,128)(2,1)}, u32[]{:S(2)}) copy-start(bf16[256,1024]{1,0:T(8,128)(2,1)} %copy-done.13) | copy-start | bytes 1572868
  60.7 9.8 %collective-permute-start.19 = (bf16[2,256,512]{2,1,0:T(8,128)(2,1)S(1)}, bf16[2,256,512]{2,1,0:T(8,128)(2,1)S(1)}, u32[]{:S(2)}, u32[]{:S(2)}) collective-permute-start(bf16[2,256,512]{2,1,0:T(8,128)(2,1)S(1)} %get-tuple-element.68), channel_id=1, source_target_pairs={{0,6},{1,25},{2,0},{3,27},{4,2},{5,29},{6,4},{7,31},{8,14},{9,1},{... | collective-permute-start | bytes 1572872 | tf_op jit(solution)/shard_map/ppermute | solution.py:36
  61.6 16.8 %collective-permute-start.20 = (bf16[2,256,512]{2,1,0:T(8,128)(2,1)S(1)}, bf16[2,256,512]{2,1,0:T(8,128)(2,1)S(1)}, u32[]{:S(2)}, u32[]{:S(2)}) collective-permute-start(bf16[2,256,512]{2,1,0:T(8,128)(2,1)S(1)} %get-tuple-element.72), channel_id=1, source_target_pairs={{0,2},{1,9},{2,4},{3,11},{4,6},{5,13},{6,0},{7,15},{8,10},{9,17},{... | collective-permute-start | bytes 1572872 | tf_op jit(solution)/shard_map/ppermute | solution.py:36
  64.0 13.6 %collective-permute-start.18 = (bf16[2,256,512]{2,1,0:T(8,128)(2,1)S(1)}, bf16[2,256,512]{2,1,0:T(8,128)(2,1)S(1)}, u32[]{:S(2)}, u32[]{:S(2)}) collective-permute-start(bf16[2,256,512]{2,1,0:T(8,128)(2,1)S(1)} %add_convert_fusion.1), channel_id=1, source_target_pairs={{0,2},{1,9},{2,4},{3,11},{4,6},{5,13},{6,0},{7,15},{8,10},{9,17},{... | collective-permute-start | bytes 1572872 | tf_op jit(solution)/shard_map/ppermute | solution.py:36
  65.5 13.0 %collective-permute-start.22 = (bf16[2,256,512]{2,1,0:T(8,128)(2,1)S(1)}, bf16[2,256,512]{2,1,0:T(8,128)(2,1)S(1)}, u32[]{:S(2)}, u32[]{:S(2)}) collective-permute-start(bf16[2,256,512]{2,1,0:T(8,128)(2,1)S(1)} %add_convert_fusion), channel_id=1, source_target_pairs={{0,6},{1,25},{2,0},{3,27},{4,2},{5,29},{6,4},{7,31},{8,14},{9,1},{... | collective-permute-start | bytes 1572872 | tf_op jit(solution)/shard_map/ppermute | solution.py:36
  77.8 8.3 %collective-permute-start.24 = (bf16[256,512]{1,0:T(8,128)(2,1)S(1)}, bf16[256,512]{1,0:T(8,128)(2,1)S(1)}, u32[]{:S(2)}, u32[]{:S(2)}) collective-permute-start(bf16[256,512]{1,0:T(8,128)(2,1)S(1)} %get-tuple-element.77), channel_id=1, source_target_pairs={{0,8},{1,3},{2,10},{3,5},{4,12},{5,7},{6,14},{7,1},{8,16},{9,11},{... | collective-permute-start | bytes 786440 | tf_op jit(solution)/shard_map/ppermute | solution.py:36
  78.6 9.3 %collective-permute-start.23 = (bf16[256,512]{1,0:T(8,128)(2,1)S(1)}, bf16[256,512]{1,0:T(8,128)(2,1)S(1)}, u32[]{:S(2)}, u32[]{:S(2)}) collective-permute-start(bf16[256,512]{1,0:T(8,128)(2,1)S(1)} %get-tuple-element.75), channel_id=1, source_target_pairs={{0,16},{1,5},{2,18},{3,7},{4,20},{5,1},{6,22},{7,3},{8,24},{9,13},... | collective-permute-start | bytes 786440 | tf_op jit(solution)/shard_map/ppermute | solution.py:36
  83.5 26.9 %copy-start.16 = (f32[1024,1,1,16]{0,3,2,1:T(8,128)S(1)}, f32[1024,1,1,16]{0,3,2,1:T(8,128)}, u32[]{:S(2)}) copy-start(f32[1024,1,1,16]{0,3,2,1:T(8,128)} %param.12) | copy-start | bytes 196612
  83.5 26.9 %copy-start.17 = (f32[1024,1,1,16]{0,3,2,1:T(8,128)S(1)}, f32[1024,1,1,16]{0,3,2,1:T(8,128)}, u32[]{:S(2)}) copy-start(f32[1024,1,1,16]{0,3,2,1:T(8,128)} %param.11) | copy-start | bytes 196612
  83.5 7.2 %collective-permute-start.25 = (bf16[256,512]{1,0:T(8,128)(2,1)S(1)}, bf16[256,512]{1,0:T(8,128)(2,1)S(1)}, u32[]{:S(2)}, u32[]{:S(2)}) collective-permute-start(bf16[256,512]{1,0:T(8,128)(2,1)S(1)} %get-tuple-element.76), channel_id=1, source_target_pairs={{0,24},{1,7},{2,26},{3,1},{4,28},{5,3},{6,30},{7,5},{8,0},{9,15},{... | collective-permute-start | bytes 786440 | tf_op jit(solution)/shard_map/ppermute | solution.py:36
  86.1 50.5 %copy-start.3 = (bf16[4096,256]{1,0:T(8,128)(2,1)S(1)}, bf16[4096,256]{1,0:T(8,128)(2,1)}, u32[]{:S(2)}) copy-start(bf16[4096,256]{1,0:T(8,128)(2,1)} %weight.1) | copy-start | bytes 6291460

commit v2 on v1

--- a/solution.py
+++ b/solution.py
@@ -369,9 +369,11 @@
         swap(y1), swap(x2), ring_y(x2), ring_x(x2), early, x2, y1, cotangent
     )
     late = project(table, 1, *both, [x2, s_x2, y1, s_y1, x3, y2])
-    other_cotangent, s_x3, s_y2, y3, late, x3, y2 = together(
-        swap(cotangent), swap(x3), swap(y2), ring_y(x3), late, x3, y2
-    )
+    top = x3.shape[0] // 2
+    other_cotangent, s_x3, s_y2, y3_top, y3_bottom, late, x3, y2 = together(
+        swap(cotangent), swap(x3), swap(y2), ring_y(x3[:top]), ring_x(y2[top:]), late, x3, y2
+    )
+    y3 = jnp.concatenate([y3_top, y3_bottom], axis=0)
     s_y3 = swap(y3)
     projected, *opposite_own = finish(
         table, *both, (s_x3, s_y2, y3, s_y3), (early, late), cotangent, other_cotangent

time: 141 us -> 140 us (level)
    ppermute x26 -> x27, waiting for transfers between devices: 33.6 us -> 32.5 us  [route(): return lax.ppermute(value, AXES, sorted(pairs))]
    ppermute x26 -> x27, starting transfers between devices: 30.2 us -> 30.4 us  [route(): return lax.ppermute(value, AXES, sorted(pairs))]
  transfers between devices with their start and end apart: 26 -> 27, of which waited for: 12 -> 12; matrix products, arithmetic and copies ran while one was open for 1% -> 1% of each run, Pallas kernels for 13% -> 13%
where the time goes in v2:
time: 140 us
  blocking collectives  44.7 us (32%)
  waiting for transfers between devices  32.5 us (23%)
  starting transfers between devices  30.4 us (22%)
  Pallas kernels  27.8 us (20%)
  local copies, waits for them, and re-layouts  1.9 us (1%)
  other arithmetic  1.54 us (1%)
    ppermute x27, waiting for transfers between devices, route(): return lax.ppermute(value, AXES, sorted(pairs))  32.5 us
    ppermute x27, starting transfers between devices, route(): return lax.ppermute(value, AXES, sorted(pairs))  30.4 us
    pallas_call x6, Pallas kernels, run(): pl.pallas_call(kernel, grid_spec=pltpu.PrefetchScalarGridSpec(num_scalar_...  27.8 us
    all_to_all x1, blocking collectives, body(): lax.all_to_all(copies, 'dp', 0, 0, tiled=True).reshape(16 * owned, low_rank)  25.4 us
    all_to_all x1, blocking collectives, exchange(): lax.all_to_all(value, AXES, 0, 0, tiled=True, axis_index_groups=groups)  19.3 us
  transfers between devices with their start and end apart: 27, of which 12 were waited for; matrix products, arithmetic and copies ran while one was open for 1% of the time, Pallas kernels for 13%

profile of v2, /device:TPU:8, one launch (start us, length us, event | category | flops | bytes accessed | tf_op | source)
XLA Modules:
  0.0 140.0 jit_solution(8292879818098637895)
XLA Ops:
  0.7 1.6 %collective-permute-start.3 = (bf16[256,1024]{1,0:T(8,128)(2,1)}, bf16[256,1024]{1,0:T(8,128)(2,1)S(1)}, u32[]{:S(2)}, u32[]{:S(2)}) collective-permute-start(bf16[256,1024]{1,0:T(8,128)(2,1)} %refs_0_.3), channel_id=1, source_target_pairs={{0,2},{1,7},{2,4},{3,1},{4,6},{5,3},{6,0},{7,5},{8,10},{9,15},{10,... | collective-permute-start | bytes 1572872 | tf_op jit(solution)/shard_map/ppermute | solution.py:36
  2.3 1.6 %collective-permute-start.2 = (bf16[256,1024]{1,0:T(8,128)(2,1)}, bf16[256,1024]{1,0:T(8,128)(2,1)S(1)}, u32[]{:S(2)}, u32[]{:S(2)}) collective-permute-start(bf16[256,1024]{1,0:T(8,128)(2,1)} %refs_0_.3), channel_id=1, source_target_pairs={{0,8},{1,25},{2,10},{3,27},{4,12},{5,29},{6,14},{7,31},{8,16},{9,1... | collective-permute-start | bytes 1572872 | tf_op jit(solution)/shard_map/ppermute | solution.py:36
  3.9 7.5 %collective-permute-done.3.refs_2_.refs_1_ = bf16[256,1024]{1,0:T(8,128)(2,1)S(1)} collective-permute-done((bf16[256,1024]{1,0:T(8,128)(2,1)}, bf16[256,1024]{1,0:T(8,128)(2,1)S(1)}, u32[]{:S(2)}, u32[]{:S(2)}) %collective-permute-start.3) | collective-permute-done | bytes 524320 | tf_op jit(solution)/shard_map/ppermute | solution.py:36
  11.4 0.3 collective-permute-done.2.refs_4_
  11.7 0.3 collective-permute-start.4
  12.0 1.3 collective-permute-start.7
  13.4 1.6 %collective-permute-start.6 = (bf16[256,1024]{1,0:T(8,128)(2,1)S(1)}, bf16[256,1024]{1,0:T(8,128)(2,1)}, u32[]{:S(2)}, u32[]{:S(2)}) collective-permute-start(bf16[256,1024]{1,0:T(8,128)(2,1)S(1)} %collective-permute-done.3.refs_2_.refs_1_), channel_id=1, source_target_pairs={{0,8},{1,25},{2,10},{3,27},{4,12},{5,29},{6,14},{7,31},{8,16},{9,1... | collective-permute-start | bytes 1572872 | tf_op jit(solution)/shard_map/ppermute | solution.py:36
  15.0 1.9 %collective-permute-start.5 = (bf16[256,1024]{1,0:T(8,128)(2,1)S(1)}, bf16[256,1024]{1,0:T(8,128)(2,1)S(1)}, u32[]{:S(2)}, u32[]{:S(2)}) collective-permute-start(bf16[256,1024]{1,0:T(8,128)(2,1)S(1)} %collective-permute-done.3.refs_2_.refs_1_), channel_id=1, source_target_pairs={{0,1},{1,0},{2,3},{3,2},{4,5},{5,4},{6,7},{7,6},{8,9},{9,8},{10,11... | collective-permute-start | bytes 1572872 | tf_op jit(solution)/shard_map/ppermute | solution.py:36
  16.9 5.7 %collective-permute-done.7.refs_0_.refs_2_ = bf16[256,1024]{1,0:T(8,128)(2,1)} collective-permute-done((bf16[256,1024]{1,0:T(8,128)(2,1)S(1)}, bf16[256,1024]{1,0:T(8,128)(2,1)}, u32[]{:S(2)}, u32[]{:S(2)}) %collective-permute-start.7) | collective-permute-done | bytes 524320 | tf_op jit(solution)/shard_map/ppermute | solution.py:36
  22.5 0.1 collective-permute-done.6.refs_2_.refs_5_
  22.7 0.3 collective-permute-start.8
  23.0 0.5 copy-done.13
  23.5 1.2 collective-permute-start.11
  24.7 1.6 %collective-permute-start.10 = (bf16[256,1024]{1,0:T(8,128)(2,1)}, bf16[256,1024]{1,0:T(8,128)(2,1)S(1)}, u32[]{:S(2)}, u32[]{:S(2)}) collective-permute-start(bf16[256,1024]{1,0:T(8,128)(2,1)} %collective-permute-done.7.refs_0_.refs_2_), channel_id=1, source_target_pairs={{0,8},{1,25},{2,10},{3,27},{4,12},{5,29},{6,14},{7,31},{8,16},{9,1... | collective-permute-start | bytes 1572872 | tf_op jit(solution)/shard_map/ppermute | solution.py:36
  26.3 1.3 collective-permute-start.9
  27.6 1.2 dynamic-slice_bitcast_fusion.table
  28.8 6.3 %shard_map.94.refs_4_ = f32[1024,512]{1,0:T(8,128)} custom-call(s32[65]{0:T(128)} %dynamic-slice_bitcast_fusion.table, bf16[512,4096]{1,0:T(8,128)(2,1)} %own.5, bf16[512,4096]{1,0:T(8,128)(2,1)} %collective-permute-done.other, bf16[256,1024]{1,0:T(8,128)(2,1)} %refs_0_.3, bf16[256,1024]{1,0:T(8,128)(2,1)} %copy-done.9, bf16[256,1024]{1,0:T(8,128)(2,1)} %copy-done.5, ...), custom_call_target="tpu_custom_call" | custom-call | flops 1610612736 | bytes 6291456 | tf_op jit(solution)/shard_map/pallas_call | solution.py:85
  35.3 0.5 collective-permute-start.13
  36.0 1.9 %collective-permute-start.16 = (bf16[128,1024]{1,0:T(8,128)(2,1)S(1)}, bf16[128,1024]{1,0:T(8,128)(2,1)S(1)}, u32[]{:S(2)}, u32[]{:S(2)}) collective-permute-start(bf16[128,1024]{1,0:T(8,128)(2,1)S(1)} %slice.43), channel_id=1, source_target_pairs={{0,2},{1,7},{2,4},{3,1},{4,6},{5,3},{6,0},{7,5},{8,10},{9,15},{10,... | collective-permute-start | bytes 786440 | tf_op jit(solution)/shard_map/ppermute | solution.py:36
  37.9 4.9 %shard_map.95.refs_5_ = f32[1024,512]{1,0:T(8,128)S(1)} custom-call(s32[65]{0:T(128)S(1)} %copy-done.15, bf16[512,4096]{1,0:T(8,128)(2,1)S(1)} %copy-done, bf16[512,4096]{1,0:T(8,128)(2,1)} %collective-permute-done.other, bf16[256,1024]{1,0:T(8,128)(2,1)} %collective-permute-done.7.refs_0_.refs_2_, ...), custom_call_target="tpu_custom_call" | custom-call | flops 1610612736 | bytes 6291456 | tf_op jit(solution)/shard_map/pallas_call | solution.py:85
  42.8 0.8 collective-permute-done.16
  43.6 1.8 %collective-permute-done.15 = bf16[128,1024]{1,0:T(8,128)(2,1)S(1)} collective-permute-done((bf16[128,1024]{1,0:T(8,128)(2,1)S(1)}, bf16[128,1024]{1,0:T(8,128)(2,1)S(1)}, u32[]{:S(2)}, u32[]{:S(2)}) %collective-permute-start.15) | collective-permute-done | bytes 262176 | tf_op jit(solution)/shard_map/ppermute | solution.py:36
  45.5 0.5 collective-permute-start.17
  46.0 1.5 %collective-permute-done.17.refs_13_.refs_3_ = bf16[256,1024]{1,0:T(8,128)(2,1)S(1)} collective-permute-done((bf16[256,1024]{1,0:T(8,128)(2,1)S(1)}, bf16[256,1024]{1,0:T(8,128)(2,1)S(1)}, u32[]{:S(2)}, u32[]{:S(2)}) %collective-permute-start.17) | collective-permute-done | bytes 524320 | tf_op jit(solution)/shard_map/ppermute | solution.py:36
  47.5 6.3 %shard_map.97 = (bf16[1024,512]{1,0:T(8,128)(2,1)S(1)}, bf16[2,256,512]{2,1,0:T(8,128)(2,1)S(1)}, bf16[2,256,512]{2,1,0:T(8,128)(2,1)S(1)}, bf16[2,256,512]{2,1,0:T(8,128)(2,1)S(1)}, bf16[2,256,512]{2,1,0:T(8,128)(2,1)S(1)}) custom-call(s32[65]{0:T(128)S(1)} %copy-done.15, bf16[512,4096]{1,0:T(8,128)(2,1)S(1)} %copy-done, ...), custom_call_target="tpu_custom_call" | custom-call | flops 2147483648 | bytes 11534336 | tf_op jit(solution)/shard_map/pallas_call | solution.py:85
  53.8 0.8 collective-permute-start.18
  54.6 2.5 %collective-permute-start.22 = (bf16[2,256,512]{2,1,0:T(8,128)(2,1)S(1)}, bf16[2,256,512]{2,1,0:T(8,128)(2,1)S(1)}, u32[]{:S(2)}, u32[]{:S(2)}) collective-permute-start(bf16[2,256,512]{2,1,0:T(8,128)(2,1)S(1)} %get-tuple-element.76), channel_id=1, source_target_pairs={{0,6},{1,25},{2,0},{3,27},{4,2},{5,29},{6,4},{7,31},{8,14},{9,1},{... | collective-permute-start | bytes 1572872 | tf_op jit(solution)/shard_map/ppermute | solution.py:36
  57.2 3.8 %shard_map.98 = (bf16[2,256,512]{2,1,0:T(8,128)(2,1)S(1)}, bf16[2,256,512]{2,1,0:T(8,128)(2,1)S(1)}, bf16[2,256,512]{2,1,0:T(8,128)(2,1)S(1)}, bf16[2,256,512]{2,1,0:T(8,128)(2,1)S(1)}) custom-call(s32[65]{0:T(128)S(1)} %copy-done.15, bf16[512,4096]{1,0:T(8,128)(2,1)S(1)} %copy-done.1, bf16[512,4096]{1,0:T(8,128)(2,1)S(1)} %collective-permute-done.12.refs_7_.far, ...), custom_call_target="tpu_custom_call" | custom-call | flops 2147483648 | bytes 7340032 | tf_op jit(solution)/shard_map/pallas_call | solution.py:85
  61.2 2.0 %collective-permute-start.21 = (bf16[2,256,512]{2,1,0:T(8,128)(2,1)S(1)}, bf16[2,256,512]{2,1,0:T(8,128)(2,1)S(1)}, u32[]{:S(2)}, u32[]{:S(2)}) collective-permute-start(bf16[2,256,512]{2,1,0:T(8,128)(2,1)S(1)} %get-tuple-element.74), channel_id=1, source_target_pairs={{0,2},{1,9},{2,4},{3,11},{4,6},{5,13},{6,0},{7,15},{8,10},{9,17},{... | collective-permute-start | bytes 1572872 | tf_op jit(solution)/shard_map/ppermute | solution.py:36
  63.2 1.1 collective-permute-done.18
  64.3 0.1 add_convert_fusion.1
  64.4 0.3 collective-permute-start.19
  64.8 0.1 add_convert_fusion
  64.9 3.3 %collective-permute-start.23 = (bf16[2,256,512]{2,1,0:T(8,128)(2,1)S(1)}, bf16[2,256,512]{2,1,0:T(8,128)(2,1)S(1)}, u32[]{:S(2)}, u32[]{:S(2)}) collective-permute-start(bf16[2,256,512]{2,1,0:T(8,128)(2,1)S(1)} %add_convert_fusion), channel_id=1, source_target_pairs={{0,6},{1,25},{2,0},{3,27},{4,2},{5,29},{6,4},{7,31},{8,14},{9,1},{... | collective-permute-start | bytes 1572872 | tf_op jit(solution)/shard_map/ppermute | solution.py:36
  68.2 2.1 %collective-permute-done.20 = bf16[2,256,512]{2,1,0:T(8,128)(2,1)S(1)} collective-permute-done((bf16[2,256,512]{2,1,0:T(8,128)(2,1)S(1)}, bf16[2,256,512]{2,1,0:T(8,128)(2,1)S(1)}, u32[]{:S(2)}, u32[]{:S(2)}) %collective-permute-start.20) | collective-permute-done | bytes 524320 | tf_op jit(solution)/shard_map/ppermute | solution.py:36
  70.3 6.9 %collective-permute-done.19 = bf16[2,256,512]{2,1,0:T(8,128)(2,1)S(1)} collective-permute-done((bf16[2,256,512]{2,1,0:T(8,128)(2,1)S(1)}, bf16[2,256,512]{2,1,0:T(8,128)(2,1)S(1)}, u32[]{:S(2)}, u32[]{:S(2)}) %collective-permute-start.19) | collective-permute-done | bytes 524320 | tf_op jit(solution)/shard_map/ppermute | solution.py:36
  77.2 0.2 fusion.2
  77.4 0.9 collective-permute-start.25
  78.3 0.2 fusion.1
  78.6 4.5 %collective-permute-start.24 = (bf16[256,512]{1,0:T(8,128)(2,1)S(1)}, bf16[256,512]{1,0:T(8,128)(2,1)S(1)}, u32[]{:S(2)}, u32[]{:S(2)}) collective-permute-start(bf16[256,512]{1,0:T(8,128)(2,1)S(1)} %get-tuple-element.77), channel_id=1, source_target_pairs={{0,16},{1,5},{2,18},{3,7},{4,20},{5,1},{6,22},{7,3},{8,24},{9,13},... | collective-permute-start | bytes 786440 | tf_op jit(solution)/shard_map/ppermute | solution.py:36
  83.2 2.5 %shard_map.96.rows = bf16[4096,1024]{1,0:T(8,128)(2,1)S(1)} custom-call(s32[65]{0:T(128)S(1)} %copy-done.15, bf16[256,1024]{1,0:T(8,128)(2,1)S(1)} %copy-done.4, bf16[256,1024]{1,0:T(8,128)(2,1)S(1)} %copy-done.6, bf16[256,1024]{1,0:T(8,128)(2,1)} %collective-permute-done.7.refs_0_.refs_2_, bf16[256,1024]{1,0:T(8,128)(2,1)S(1)} %collective-permute-done.11.refs_4_.refs_3_, ...), custom_call_target="tpu_custom_call" | custom-call | bytes 16777216 | tf_op jit(solution)/shard_map/pallas_call | solution.py:85
  85.7 1.9 %collective-permute-done.24 = bf16[256,512]{1,0:T(8,128)(2,1)S(1)} collective-permute-done((bf16[256,512]{1,0:T(8,128)(2,1)S(1)}, bf16[256,512]{1,0:T(8,128)(2,1)S(1)}, u32[]{:S(2)}, u32[]{:S(2)}) %collective-permute-start.24) | collective-permute-done | bytes 262176 | tf_op jit(solution)/shard_map/ppermute | solution.py:36
  87.5 2.7 %collective-permute-done.26 = bf16[256,512]{1,0:T(8,128)(2,1)S(1)} collective-permute-done((bf16[256,512]{1,0:T(8,128)(2,1)S(1)}, bf16[256,512]{1,0:T(8,128)(2,1)S(1)}, u32[]{:S(2)}, u32[]{:S(2)}) %collective-permute-start.26) | collective-permute-done | bytes 262176 | tf_op jit(solution)/shard_map/ppermute | solution.py:36
  90.3 0.1 add_convert_fusion.2
  90.4 19.3 %all_to_all.10 = bf16[16,16,512]{2,1,0:T(8,128)(2,1)S(1)} all-to-all(bf16[16,16,512]{2,1,0:T(8,128)(2,1)S(1)} %bitcast.42), channel_id=1, replica_groups={{0,1,32,33,64,65,96,97,128,129,160,161,192,193,224,225},{2,3,34,35,66,6..., dimensions={0} | all-to-all | bytes 524288 | tf_op jit(solution)/shard_map/all_to_all | solution.py:71
  109.8 0.7 fusion.6
  110.5 25.4 %all_to_all.11 = bf16[16,16,1024]{2,1,0:T(8,128)(2,1)S(1)} all-to-all(bf16[16,16,1024]{2,1,0:T(8,128)(2,1)S(1)} %broadcast_in_dim.2), channel_id=1, replica_groups=mesh['dp'=16,'fsdp'=16] {'dp'}, dimensions={0} | all-to-all | bytes 1048576 | tf_op jit(solution)/shard_map/all_to_all | solution.py:413
  135.9 4.0 %shard_map.99 = bf16[4096,256]{1,0:T(8,128)(2,1)} custom-call(s32[65]{0:T(128)S(1)} %copy-done.15, bf16[4096,1024]{1,0:T(8,128)(2,1)S(1)} %shard_map.96.rows, bf16[256,1024]{1,0:T(8,128)(2,1)S(1)} %bitcast.41, bf16[4096,256]{1,0:T(8,128)(2,1)S(1)} %copy-done.3), custom_call_target="tpu_custom_call" | custom-call | flops 2147483648 | bytes 13631488 | tf_op jit(solution)/shard_map/pallas_call | solution.py:85
  (64 shorter events, 0.7 us)
Async XLA Ops:
  0.6 11.1 %collective-permute-start = (bf16[512,4096]{1,0:T(8,128)(2,1)}, bf16[512,4096]{1,0:T(8,128)(2,1)}, u32[]{:S(2)}, u32[]{:S(2)}) collective-permute-start(bf16[512,4096]{1,0:T(8,128)(2,1)} %own.5), channel_id=1, source_target_pairs={{0,1},{1,0},{2,3},{3,2},{4,5},{5,4},{6,7},{7,6},{8,9},{9,8},{10,11... | collective-permute-start | bytes 12582920 | tf_op jit(solution)/shard_map/ppermute | solution.py:36
  0.7 10.7 %collective-permute-start.3 = (bf16[256,1024]{1,0:T(8,128)(2,1)}, bf16[256,1024]{1,0:T(8,128)(2,1)S(1)}, u32[]{:S(2)}, u32[]{:S(2)}) collective-permute-start(bf16[256,1024]{1,0:T(8,128)(2,1)} %refs_0_.3), channel_id=1, source_target_pairs={{0,2},{1,7},{2,4},{3,1},{4,6},{5,3},{6,0},{7,5},{8,10},{9,15},{10,... | collective-permute-start | bytes 1572872 | tf_op jit(solution)/shard_map/ppermute | solution.py:36
  2.3 9.4 %collective-permute-start.2 = (bf16[256,1024]{1,0:T(8,128)(2,1)}, bf16[256,1024]{1,0:T(8,128)(2,1)S(1)}, u32[]{:S(2)}, u32[]{:S(2)}) collective-permute-start(bf16[256,1024]{1,0:T(8,128)(2,1)} %refs_0_.3), channel_id=1, source_target_pairs={{0,8},{1,25},{2,10},{3,27},{4,12},{5,29},{6,14},{7,31},{8,16},{9,1... | collective-permute-start | bytes 1572872 | tf_op jit(solution)/shard_map/ppermute | solution.py:36
  3.9 7.8 %collective-permute-start.1 = (bf16[256,1024]{1,0:T(8,128)(2,1)}, bf16[256,1024]{1,0:T(8,128)(2,1)S(1)}, u32[]{:S(2)}, u32[]{:S(2)}) collective-permute-start(bf16[256,1024]{1,0:T(8,128)(2,1)} %refs_0_.3), channel_id=1, source_target_pairs={{0,1},{1,0},{2,3},{3,2},{4,5},{5,4},{6,7},{7,6},{8,9},{9,8},{10,11... | collective-permute-start | bytes 1572872 | tf_op jit(solution)/shard_map/ppermute | solution.py:36
  11.4 17.4 %copy-start.5 = (bf16[256,1024]{1,0:T(8,128)(2,1)}, bf16[256,1024]{1,0:T(8,128)(2,1)S(1)}, u32[]{:S(2)}) copy-start(bf16[256,1024]{1,0:T(8,128)(2,1)S(1)} %collective-permute-done.3.refs_2_.refs_1_) | copy-start | bytes 1572868
  11.7 17.1 %copy-start.7 = (bf16[256,1024]{1,0:T(8,128)(2,1)}, bf16[256,1024]{1,0:T(8,128)(2,1)S(1)}, u32[]{:S(2)}) copy-start(bf16[256,1024]{1,0:T(8,128)(2,1)S(1)} %collective-permute-done.2.refs_4_) | copy-start | bytes 1572868
  11.7 17.1 %copy-start.9 = (bf16[256,1024]{1,0:T(8,128)(2,1)}, bf16[256,1024]{1,0:T(8,128)(2,1)S(1)}, u32[]{:S(2)}) copy-start(bf16[256,1024]{1,0:T(8,128)(2,1)S(1)} %collective-permute-done.1.refs_1_.refs_8_) | copy-start | bytes 1572868
  11.7 5.2 %collective-permute-start.4 = (bf16[256,1024]{1,0:T(8,128)(2,1)S(1)}, bf16[256,1024]{1,0:T(8,128)(2,1)S(1)}, u32[]{:S(2)}, u32[]{:S(2)}) collective-permute-start(bf16[256,1024]{1,0:T(8,128)(2,1)S(1)} %collective-permute-done.2.refs_4_), channel_id=1, source_target_pairs={{0,1},{1,0},{2,3},{3,2},{4,5},{5,4},{6,7},{7,6},{8,9},{9,8},{10,11... | collective-permute-start | bytes 1572872 | tf_op jit(solution)/shard_map/ppermute | solution.py:36
  12.0 10.5 %collective-permute-start.7 = (bf16[256,1024]{1,0:T(8,128)(2,1)S(1)}, bf16[256,1024]{1,0:T(8,128)(2,1)}, u32[]{:S(2)}, u32[]{:S(2)}) collective-permute-start(bf16[256,1024]{1,0:T(8,128)(2,1)S(1)} %collective-permute-done.3.refs_2_.refs_1_), channel_id=1, source_target_pairs={{0,2},{1,7},{2,4},{3,1},{4,6},{5,3},{6,0},{7,5},{8,10},{9,15},{10,... | collective-permute-start | bytes 1572872 | tf_op jit(solution)/shard_map/ppermute | solution.py:36
  13.4 9.3 %collective-permute-start.6 = (bf16[256,1024]{1,0:T(8,128)(2,1)S(1)}, bf16[256,1024]{1,0:T(8,128)(2,1)}, u32[]{:S(2)}, u32[]{:S(2)}) collective-permute-start(bf16[256,1024]{1,0:T(8,128)(2,1)S(1)} %collective-permute-done.3.refs_2_.refs_1_), channel_id=1, source_target_pairs={{0,8},{1,25},{2,10},{3,27},{4,12},{5,29},{6,14},{7,31},{8,16},{9,1... | collective-permute-start | bytes 1572872 | tf_op jit(solution)/shard_map/ppermute | solution.py:36
  15.0 7.7 %collective-permute-start.5 = (bf16[256,1024]{1,0:T(8,128)(2,1)S(1)}, bf16[256,1024]{1,0:T(8,128)(2,1)S(1)}, u32[]{:S(2)}, u32[]{:S(2)}) collective-permute-start(bf16[256,1024]{1,0:T(8,128)(2,1)S(1)} %collective-permute-done.3.refs_2_.refs_1_), channel_id=1, source_target_pairs={{0,1},{1,0},{2,3},{3,2},{4,5},{5,4},{6,7},{7,6},{8,9},{9,8},{10,11... | collective-permute-start | bytes 1572872 | tf_op jit(solution)/shard_map/ppermute | solution.py:36
  16.9 11.9 %copy-start.11 = (bf16[256,1024]{1,0:T(8,128)(2,1)}, bf16[256,1024]{1,0:T(8,128)(2,1)S(1)}, u32[]{:S(2)}) copy-start(bf16[256,1024]{1,0:T(8,128)(2,1)S(1)} %collective-permute-done.4.refs_5_.refs_12_) | copy-start | bytes 1572868
  22.7 0.8 copy-start.13
  22.7 12.5 %collective-permute-start.8 = (bf16[256,1024]{1,0:T(8,128)(2,1)}, bf16[256,1024]{1,0:T(8,128)(2,1)}, u32[]{:S(2)}, u32[]{:S(2)}) collective-permute-start(bf16[256,1024]{1,0:T(8,128)(2,1)} %collective-permute-done.6.refs_2_.refs_5_), channel_id=1, source_target_pairs={{0,1},{1,0},{2,3},{3,2},{4,5},{5,4},{6,7},{7,6},{8,9},{9,8},{10,11... | collective-permute-start | bytes 1572872 | tf_op jit(solution)/shard_map/ppermute | solution.py:36
  23.5 11.6 %collective-permute-start.11 = (bf16[256,1024]{1,0:T(8,128)(2,1)}, bf16[256,1024]{1,0:T(8,128)(2,1)S(1)}, u32[]{:S(2)}, u32[]{:S(2)}) collective-permute-start(bf16[256,1024]{1,0:T(8,128)(2,1)} %collective-permute-done.7.refs_0_.refs_2_), channel_id=1, source_target_pairs={{0,2},{1,7},{2,4},{3,1},{4,6},{5,3},{6,0},{7,5},{8,10},{9,15},{10,... | collective-permute-start | bytes 1572872 | tf_op jit(solution)/shard_map/ppermute | solution.py:36
  24.7 10.5 %collective-permute-start.10 = (bf16[256,1024]{1,0:T(8,128)(2,1)}, bf16[256,1024]{1,0:T(8,128)(2,1)S(1)}, u32[]{:S(2)}, u32[]{:S(2)}) collective-permute-start(bf16[256,1024]{1,0:T(8,128)(2,1)} %collective-permute-done.7.refs_0_.refs_2_), channel_id=1, source_target_pairs={{0,8},{1,25},{2,10},{3,27},{4,12},{5,29},{6,14},{7,31},{8,16},{9,1... | collective-permute-start | bytes 1572872 | tf_op jit(solution)/shard_map/ppermute | solution.py:36
  26.3 8.9 %collective-permute-start.9 = (bf16[256,1024]{1,0:T(8,128)(2,1)}, bf16[256,1024]{1,0:T(8,128)(2,1)}, u32[]{:S(2)}, u32[]{:S(2)}) collective-permute-start(bf16[256,1024]{1,0:T(8,128)(2,1)} %collective-permute-done.7.refs_0_.refs_2_), channel_id=1, source_target_pairs={{0,1},{1,0},{2,3},{3,2},{4,5},{5,4},{6,7},{7,6},{8,9},{9,8},{10,11... | collective-permute-start | bytes 1572872 | tf_op jit(solution)/shard_map/ppermute | solution.py:36
  28.8 9.1 %copy-start = (bf16[512,4096]{1,0:T(8,128)(2,1)S(1)}, bf16[512,4096]{1,0:T(8,128)(2,1)}, u32[]{:S(2)}) copy-start(bf16[512,4096]{1,0:T(8,128)(2,1)} %own.5) | copy-start | bytes 12582916
  28.8 9.1 %copy-start.15 = (s32[65]{0:T(128)S(1)}, s32[65]{0:T(128)}, u32[]{:S(2)}) copy-start(s32[65]{0:T(128)} %dynamic-slice_bitcast_fusion.table) | copy-start | bytes 784
  35.2 10.2 %collective-permute-start.12 = (bf16[512,4096]{1,0:T(8,128)(2,1)}, bf16[512,4096]{1,0:T(8,128)(2,1)S(1)}, u32[]{:S(2)}, u32[]{:S(2)}) collective-permute-start(bf16[512,4096]{1,0:T(8,128)(2,1)} %near), channel_id=1, source_target_pairs={{0,1},{1,0},{2,3},{3,2},{4,5},{5,4},{6,7},{7,6},{8,9},{9,8},{10,11... | collective-permute-start | bytes 12582920 | tf_op jit(solution)/shard_map/ppermute | solution.py:36
  35.3 10.1 %collective-permute-start.13 = (bf16[256,1024]{1,0:T(8,128)(2,1)S(1)}, bf16[256,1024]{1,0:T(8,128)(2,1)S(1)}, u32[]{:S(2)}, u32[]{:S(2)}) collective-permute-start(bf16[256,1024]{1,0:T(8,128)(2,1)S(1)} %collective-permute-done.11.refs_4_.refs_3_), channel_id=1, source_target_pairs={{0,1},{1,0},{2,3},{3,2},{4,5},{5,4},{6,7},{7,6},{8,9},{9,8},{10,11... | collective-permute-start | bytes 1572872 | tf_op jit(solution)/shard_map/ppermute | solution.py:36
  35.8 9.6 %collective-permute-start.14 = (bf16[256,1024]{1,0:T(8,128)(2,1)S(1)}, bf16[256,1024]{1,0:T(8,128)(2,1)S(1)}, u32[]{:S(2)}, u32[]{:S(2)}) collective-permute-start(bf16[256,1024]{1,0:T(8,128)(2,1)S(1)} %collective-permute-done.10.refs_5_.refs_6_), channel_id=1, source_target_pairs={{0,1},{1,0},{2,3},{3,2},{4,5},{5,4},{6,7},{7,6},{8,9},{9,8},{10,11... | collective-permute-start | bytes 1572872 | tf_op jit(solution)/shard_map/ppermute | solution.py:36
  35.9 11.6 %copy-start.1 = (bf16[512,4096]{1,0:T(8,128)(2,1)S(1)}, bf16[512,4096]{1,0:T(8,128)(2,1)}, u32[]{:S(2)}) copy-start(bf16[512,4096]{1,0:T(8,128)(2,1)} %near) | copy-start | bytes 12582916
  35.9 11.6 %copy-start.2 = (f32[1024,512]{1,0:T(8,128)S(1)}, f32[1024,512]{1,0:T(8,128)}, u32[]{:S(2)}) copy-start(f32[1024,512]{1,0:T(8,128)} %shard_map.94.refs_4_) | copy-start | bytes 6291460
  36.0 7.7 %collective-permute-start.16 = (bf16[128,1024]{1,0:T(8,128)(2,1)S(1)}, bf16[128,1024]{1,0:T(8,128)(2,1)S(1)}, u32[]{:S(2)}, u32[]{:S(2)}) collective-permute-start(bf16[128,1024]{1,0:T(8,128)(2,1)S(1)} %slice.43), channel_id=1, source_target_pairs={{0,2},{1,7},{2,4},{3,1},{4,6},{5,3},{6,0},{7,5},{8,10},{9,15},{10,... | collective-permute-start | bytes 786440 | tf_op jit(solution)/shard_map/ppermute | solution.py:36
  37.9 7.6 %collective-permute-start.15 = (bf16[128,1024]{1,0:T(8,128)(2,1)S(1)}, bf16[128,1024]{1,0:T(8,128)(2,1)S(1)}, u32[]{:S(2)}, u32[]{:S(2)}) collective-permute-start(bf16[128,1024]{1,0:T(8,128)(2,1)S(1)} %slice.42), channel_id=1, source_target_pairs={{0,8},{1,25},{2,10},{3,27},{4,12},{5,29},{6,14},{7,31},{8,16},{9,1... | collective-permute-start | bytes 786440 | tf_op jit(solution)/shard_map/ppermute | solution.py:36
  45.5 2.0 %collective-permute-start.17 = (bf16[256,1024]{1,0:T(8,128)(2,1)S(1)}, bf16[256,1024]{1,0:T(8,128)(2,1)S(1)}, u32[]{:S(2)}, u32[]{:S(2)}) collective-permute-start(bf16[256,1024]{1,0:T(8,128)(2,1)S(1)} %constant_dynamic-update-slice_fusion.refs_7_.refs_2_), channel_id=1, source_target_pairs={{0,1},{1,0},{2,3},{3,2},{4,5},{5,4},{6,7},{7,6},{8,9},{9,8},{10,11... | collective-permute-start | bytes 1572872 | tf_op jit(solution)/shard_map/ppermute | solution.py:36
  53.8 10.5 %collective-permute-start.18 = (bf16[2,256,512]{2,1,0:T(8,128)(2,1)S(1)}, bf16[2,256,512]{2,1,0:T(8,128)(2,1)S(1)}, u32[]{:S(2)}, u32[]{:S(2)}) collective-permute-start(bf16[2,256,512]{2,1,0:T(8,128)(2,1)S(1)} %get-tuple-element.69), channel_id=1, source_target_pairs={{0,2},{1,9},{2,4},{3,11},{4,6},{5,13},{6,0},{7,15},{8,10},{9,17},{... | collective-permute-start | bytes 1572872 | tf_op jit(solution)/shard_map/ppermute | solution.py:36
  54.6 10.1 %collective-permute-start.22 = (bf16[2,256,512]{2,1,0:T(8,128)(2,1)S(1)}, bf16[2,256,512]{2,1,0:T(8,128)(2,1)S(1)}, u32[]{:S(2)}, u32[]{:S(2)}) collective-permute-start(bf16[2,256,512]{2,1,0:T(8,128)(2,1)S(1)} %get-tuple-element.76), channel_id=1, source_target_pairs={{0,6},{1,25},{2,0},{3,27},{4,2},{5,29},{6,4},{7,31},{8,14},{9,1},{... | collective-permute-start | bytes 1572872 | tf_op jit(solution)/shard_map/ppermute | solution.py:36
  61.0 22.1 %copy-start.4 = (bf16[256,1024]{1,0:T(8,128)(2,1)S(1)}, bf16[256,1024]{1,0:T(8,128)(2,1)}, u32[]{:S(2)}) copy-start(bf16[256,1024]{1,0:T(8,128)(2,1)} %refs_0_.3) | copy-start | bytes 1572868
  61.0 22.1 %copy-start.6 = (bf16[256,1024]{1,0:T(8,128)(2,1)S(1)}, bf16[256,1024]{1,0:T(8,128)(2,1)}, u32[]{:S(2)}) copy-start(bf16[256,1024]{1,0:T(8,128)(2,1)} %copy-done.5) | copy-start | bytes 1572868
  61.0 22.1 %copy-start.8 = (bf16[256,1024]{1,0:T(8,128)(2,1)S(1)}, bf16[256,1024]{1,0:T(8,128)(2,1)}, u32[]{:S(2)}) copy-start(bf16[256,1024]{1,0:T(8,128)(2,1)} %copy-done.7) | copy-start | bytes 1572868
  61.0 22.1 %copy-start.10 = (bf16[256,1024]{1,0:T(8,128)(2,1)S(1)}, bf16[256,1024]{1,0:T(8,128)(2,1)}, u32[]{:S(2)}) copy-start(bf16[256,1024]{1,0:T(8,128)(2,1)} %copy-done.9) | copy-start | bytes 1572868
  61.0 22.1 %copy-start.12 = (bf16[256,1024]{1,0:T(8,128)(2,1)S(1)}, bf16[256,1024]{1,0:T(8,128)(2,1)}, u32[]{:S(2)}) copy-start(bf16[256,1024]{1,0:T(8,128)(2,1)} %copy-done.11) | copy-start | bytes 1572868
  61.1 22.1 %copy-start.14 = (bf16[256,1024]{1,0:T(8,128)(2,1)S(1)}, bf16[256,1024]{1,0:T(8,128)(2,1)}, u32[]{:S(2)}) copy-start(bf16[256,1024]{1,0:T(8,128)(2,1)} %copy-done.13) | copy-start | bytes 1572868
  61.1 9.3 %collective-permute-start.20 = (bf16[2,256,512]{2,1,0:T(8,128)(2,1)S(1)}, bf16[2,256,512]{2,1,0:T(8,128)(2,1)S(1)}, u32[]{:S(2)}, u32[]{:S(2)}) collective-permute-start(bf16[2,256,512]{2,1,0:T(8,128)(2,1)S(1)} %get-tuple-element.70), channel_id=1, source_target_pairs={{0,6},{1,25},{2,0},{3,27},{4,2},{5,29},{6,4},{7,31},{8,14},{9,1},{... | collective-permute-start | bytes 1572872 | tf_op jit(solution)/shard_map/ppermute | solution.py:36
  61.2 17.2 %collective-permute-start.21 = (bf16[2,256,512]{2,1,0:T(8,128)(2,1)S(1)}, bf16[2,256,512]{2,1,0:T(8,128)(2,1)S(1)}, u32[]{:S(2)}, u32[]{:S(2)}) collective-permute-start(bf16[2,256,512]{2,1,0:T(8,128)(2,1)S(1)} %get-tuple-element.74), channel_id=1, source_target_pairs={{0,2},{1,9},{2,4},{3,11},{4,6},{5,13},{6,0},{7,15},{8,10},{9,17},{... | collective-permute-start | bytes 1572872 | tf_op jit(solution)/shard_map/ppermute | solution.py:36
  64.4 12.8 %collective-permute-start.19 = (bf16[2,256,512]{2,1,0:T(8,128)(2,1)S(1)}, bf16[2,256,512]{2,1,0:T(8,128)(2,1)S(1)}, u32[]{:S(2)}, u32[]{:S(2)}) collective-permute-start(bf16[2,256,512]{2,1,0:T(8,128)(2,1)S(1)} %add_convert_fusion.1), channel_id=1, source_target_pairs={{0,2},{1,9},{2,4},{3,11},{4,6},{5,13},{6,0},{7,15},{8,10},{9,17},{... | collective-permute-start | bytes 1572872 | tf_op jit(solution)/shard_map/ppermute | solution.py:36
  64.9 13.4 %collective-permute-start.23 = (bf16[2,256,512]{2,1,0:T(8,128)(2,1)S(1)}, bf16[2,256,512]{2,1,0:T(8,128)(2,1)S(1)}, u32[]{:S(2)}, u32[]{:S(2)}) collective-permute-start(bf16[2,256,512]{2,1,0:T(8,128)(2,1)S(1)} %add_convert_fusion), channel_id=1, source_target_pairs={{0,6},{1,25},{2,0},{3,27},{4,2},{5,29},{6,4},{7,31},{8,14},{9,1},{... | collective-permute-start | bytes 1572872 | tf_op jit(solution)/shard_map/ppermute | solution.py:36
  77.4 8.2 %collective-permute-start.25 = (bf16[256,512]{1,0:T(8,128)(2,1)S(1)}, bf16[256,512]{1,0:T(8,128)(2,1)S(1)}, u32[]{:S(2)}, u32[]{:S(2)}) collective-permute-start(bf16[256,512]{1,0:T(8,128)(2,1)S(1)} %get-tuple-element.79), channel_id=1, source_target_pairs={{0,8},{1,3},{2,10},{3,5},{4,12},{5,7},{6,14},{7,1},{8,16},{9,11},{... | collective-permute-start | bytes 786440 | tf_op jit(solution)/shard_map/ppermute | solution.py:36
  78.6 9.0 %collective-permute-start.24 = (bf16[256,512]{1,0:T(8,128)(2,1)S(1)}, bf16[256,512]{1,0:T(8,128)(2,1)S(1)}, u32[]{:S(2)}, u32[]{:S(2)}) collective-permute-start(bf16[256,512]{1,0:T(8,128)(2,1)S(1)} %get-tuple-element.77), channel_id=1, source_target_pairs={{0,16},{1,5},{2,18},{3,7},{4,20},{5,1},{6,22},{7,3},{8,24},{9,13},... | collective-permute-start | bytes 786440 | tf_op jit(solution)/shard_map/ppermute | solution.py:36
  83.1 26.6 %copy-start.16 = (f32[1024,1,1,16]{0,3,2,1:T(8,128)S(1)}, f32[1024,1,1,16]{0,3,2,1:T(8,128)}, u32[]{:S(2)}) copy-start(f32[1024,1,1,16]{0,3,2,1:T(8,128)} %param.12) | copy-start | bytes 196612
  83.1 26.6 %copy-start.17 = (f32[1024,1,1,16]{0,3,2,1:T(8,128)S(1)}, f32[1024,1,1,16]{0,3,2,1:T(8,128)}, u32[]{:S(2)}) copy-start(f32[1024,1,1,16]{0,3,2,1:T(8,128)} %param.11) | copy-start | bytes 196612
  83.1 7.2 %collective-permute-start.26 = (bf16[256,512]{1,0:T(8,128)(2,1)S(1)}, bf16[256,512]{1,0:T(8,128)(2,1)S(1)}, u32[]{:S(2)}, u32[]{:S(2)}) collective-permute-start(bf16[256,512]{1,0:T(8,128)(2,1)S(1)} %get-tuple-element.78), channel_id=1, source_target_pairs={{0,24},{1,7},{2,26},{3,1},{4,28},{5,3},{6,30},{7,5},{8,0},{9,15},{... | collective-permute-start | bytes 786440 | tf_op jit(solution)/shard_map/ppermute | solution.py:36
  85.6 50.3 %copy-start.3 = (bf16[4096,256]{1,0:T(8,128)(2,1)S(1)}, bf16[4096,256]{1,0:T(8,128)(2,1)}, u32[]{:S(2)}) copy-start(bf16[4096,256]{1,0:T(8,128)(2,1)} %weight.1) | copy-start | bytes 6291460
